TPU v7x, 256 devices: a whole 4x4x8 slice. The times are simulated.
256 devices in a mesh: branch: 2 (over y_hi), blk: 16 (over x, y_lo, core), head: 8 (over z).
Axes of the slice: x: 4, y: 4 (y_hi: 2, y_lo: 2; y = y_hi * 2 + y_lo), z: 8, core: 2. Of those that a mesh axis runs over, the one named last changes fastest.
Arguments:
- queries: bfloat16 [2, 6144, 2048], P('branch', 'blk', 'head'), may hold values from -600 to 600
- keys: bfloat16 [2, 6144, 2048], P('branch', 'blk', 'head'), may hold values from -8 to 8
- values: bfloat16 [2, 6144, 2048], P('branch', 'blk', 'head'), may hold values from -6 to 6
- reward_grad: bfloat16 [6144, 2048], P('blk', 'head'), may hold values from -1.1953125 to 1.1953125
- qkv_weight: bfloat16 [3, 3072, 2048], P(None, None, 'head'), may hold values from -0.109375 to 0.109375
Outputs:
- latent_grad: bfloat16 [6144, 3072], P(('blk', 'head'), 'branch')
All inputs are finite; a program needn't handle non-finite values.
Results may differ from a plain program's by a relative error of at most 0.02.
Values may be sent and summed in bfloat16 or wider, within the bound.
A program may use at most 128 MiB of HBM per device.

v0:
```python
import jax
import jax.numpy as jnp
from jax import lax
from jax.sharding import PartitionSpec as P

HEAD_DIM = 128


GUIDE = 6.0


def from_behind(value, axis, steps):
    count = lax.axis_size(axis)
    pairs = [(source, (source + steps) % count) for source in range(count)]
    return lax.ppermute(value, axis, pairs)


def absorb(state, queries_here, key_block, value_block, scale):
    peak, total, accum = state
    scores = (
        jnp.einsum("qhd,khd->hqk", queries_here, key_block, preferred_element_type=jnp.float32)
        * scale
    )
    top = jnp.maximum(peak, jnp.max(scores, axis=2))
    weights = jnp.exp(scores - top[:, :, None])
    fade = jnp.exp(peak - top)
    total = total * fade + jnp.sum(weights, axis=2)
    update = jnp.einsum(
        "hqk,khd->hqd", weights, value_block.astype(jnp.float32), precision=lax.Precision.HIGHEST
    )
    accum = accum * fade[:, :, None] + update
    return (top, total, accum)


def blame(queries_here, dout_here, lse, delta, key_block, value_block, scale):
    scores = (
        jnp.einsum("qhd,khd->hqk", queries_here, key_block, preferred_element_type=jnp.float32)
        * scale
    )
    probs = jnp.exp(scores - lse[:, :, None])
    probs_low = probs.astype(jnp.bfloat16)
    dprobs = jnp.einsum("qhd,khd->hqk", dout_here, value_block, preferred_element_type=jnp.float32)
    dscores = (probs * (dprobs - delta[:, :, None])).astype(jnp.bfloat16)
    grad_v = jnp.einsum("hqk,qhd->khd", probs_low, dout_here, preferred_element_type=jnp.float32)
    grad_k = (
        jnp.einsum("hqk,qhd->khd", dscores, queries_here, preferred_element_type=jnp.float32)
        * scale
    )
    grad_q = (
        jnp.einsum("hqk,khd->qhd", dscores, key_block, preferred_element_type=jnp.float32) * scale
    )
    return (grad_q, grad_k, grad_v)


def per_device(queries, keys, values, reward_grad, qkv_weight):
    scale = HEAD_DIM ** (-0.5)
    side = lax.axis_index("branch")
    coef = jnp.where(side == 0, 1.0 - GUIDE, GUIDE).astype(jnp.float32)
    dout = (coef * reward_grad.astype(jnp.float32)).astype(jnp.bfloat16)
    rows = queries.shape[1]
    local = queries.shape[2] // HEAD_DIM
    cycle_len = lax.axis_size("blk")
    q_here = queries[0].reshape(rows, local, HEAD_DIM)
    k_here = keys[0].reshape(rows, local, HEAD_DIM)
    v_here = values[0].reshape(rows, local, HEAD_DIM)
    o_here = dout.reshape(rows, local, HEAD_DIM)
    start_state = (
        jnp.full((local, rows), -1e30, jnp.float32),
        jnp.zeros((local, rows), jnp.float32),
        jnp.zeros((local, rows, HEAD_DIM), jnp.float32),
    )

    def forward_turn(turn, carry):
        state, key_block, value_block = carry
        state = absorb(state, q_here, key_block, value_block, scale)
        key_block, value_block = from_behind((key_block, value_block), "blk", 1)
        return (state, key_block, value_block)

    state = lax.fori_loop(0, cycle_len, forward_turn, (start_state, k_here, v_here))[0]
    peak, total, accum = state
    lse = peak + jnp.log(total)
    attn_out = accum / total[:, :, None]
    delta = jnp.einsum(
        "qhd,hqd->hq", o_here.astype(jnp.float32), attn_out, precision=lax.Precision.HIGHEST
    )
    grad_zero = jnp.zeros((rows, local, HEAD_DIM), jnp.float32)

    def backward_turn(turn, carry):
        grad_q, key_block, value_block, grad_k, grad_v = carry
        part_q, part_k, part_v = blame(q_here, o_here, lse, delta, key_block, value_block, scale)
        key_block, value_block = from_behind((key_block, value_block), "blk", 1)
        grad_k, grad_v = from_behind((grad_k + part_k, grad_v + part_v), "blk", 1)
        return (grad_q + part_q, key_block, value_block, grad_k, grad_v)

    grad_q, _, _, grad_k, grad_v = lax.fori_loop(
        0, cycle_len, backward_turn, (grad_zero, k_here, v_here, grad_zero, grad_zero)
    )
    grad_qkv = (
        jnp.stack([grad_q, grad_k, grad_v]).astype(jnp.bfloat16).reshape(3, rows, local * HEAD_DIM)
    )
    mine = lax.psum_scatter(
        jnp.einsum("tqc,tdc->qd", grad_qkv, qkv_weight, preferred_element_type=jnp.float32).astype(
            jnp.bfloat16
        ),
        "head",
        scatter_dimension=0,
        tiled=True,
    )
    result = lax.psum_scatter(mine, "branch", scatter_dimension=1, tiled=True).astype(jnp.float32)
    return result.astype(jnp.bfloat16)


def solution(mesh):
    placed = (
        P("branch", "blk", "head"),
        P("branch", "blk", "head"),
        P("branch", "blk", "head"),
        P("blk", "head"),
        P(None, None, "head"),
    )
    return jax.shard_map(
        per_device,
        mesh=mesh,
        in_specs=placed,
        out_specs=P(("blk", "head"), "branch"),
        check_vma=False,
    )
```

profile of v0, /device:TPU:1, one launch (start us, length us, event | category | flops | bytes accessed | tf_op | source)
XLA Modules:
  0.0 560.4 jit_solution(3072979309746917914)
XLA Ops:
  11.3 145.7 %while.38 = (s32[]{:T(128)}, f32[2,384]{1,0:T(2,128)S(1)}, f32[2,384]{1,0:T(2,128)S(1)}, f32[2,384,128]{2,1,0:T(8,128)S(1)}, bf16[384,2,128]{2,0,1:T(8,128)(2,1)...) while((s32[]{:T(128)}, f32[2,384]{1,0:T(2,128)S(1)}, ...), condition=%wide.region_3.4_spmd.clone, body=%wide.region_0.3_spmd.clone.sunk | while | flops 530255616 | bytes 7323833 | solution.py:79
  11.3 2.8 collective-permute-start
  14.7 1.2 convolution_add_fusion.2
  16.7 2.1 collective-permute-done.1
  18.8 2.6 collective-permute-start
  23.3 1.7 collective-permute-done
  26.1 2.6 collective-permute-start
  30.6 3.8 collective-permute-done
  34.7 1.3 collective-permute-start
  38.7 5.1 collective-permute-done
  46.9 6.3 %collective-permute-done = bf16[384,2,128]{2,0,1:T(8,128)(2,1)S(1)} collective-permute-done((bf16[384,2,128]{2,0,1:T(8,128)(2,1)S(1)}, bf16[384,2,128]{2,0,1:T(8,128)(2,1)S(1)}, u32[]{:S(2)}, u32[]{:S(2)}) %collective-permute-start) | collective-permute-done | bytes 196640 | tf_op jit(solution)/shard_map/while/body/eval_jaxpr/ppermute | solution.py:15
  54.2 1.2 convolution_add_fusion.2
  55.5 7.1 %collective-permute-done = bf16[384,2,128]{2,0,1:T(8,128)(2,1)S(1)} collective-permute-done((bf16[384,2,128]{2,0,1:T(8,128)(2,1)S(1)}, bf16[384,2,128]{2,0,1:T(8,128)(2,1)S(1)}, u32[]{:S(2)}, u32[]{:S(2)}) %collective-permute-start) | collective-permute-done | bytes 196640 | tf_op jit(solution)/shard_map/while/body/eval_jaxpr/ppermute | solution.py:15
  63.7 1.2 convolution_add_fusion.2
  64.9 7.1 %collective-permute-done = bf16[384,2,128]{2,0,1:T(8,128)(2,1)S(1)} collective-permute-done((bf16[384,2,128]{2,0,1:T(8,128)(2,1)S(1)}, bf16[384,2,128]{2,0,1:T(8,128)(2,1)S(1)}, u32[]{:S(2)}, u32[]{:S(2)}) %collective-permute-start) | collective-permute-done | bytes 196640 | tf_op jit(solution)/shard_map/while/body/eval_jaxpr/ppermute | solution.py:15
  74.3 7.1 %collective-permute-done = bf16[384,2,128]{2,0,1:T(8,128)(2,1)S(1)} collective-permute-done((bf16[384,2,128]{2,0,1:T(8,128)(2,1)S(1)}, bf16[384,2,128]{2,0,1:T(8,128)(2,1)S(1)}, u32[]{:S(2)}, u32[]{:S(2)}) %collective-permute-start) | collective-permute-done | bytes 196640 | tf_op jit(solution)/shard_map/while/body/eval_jaxpr/ppermute | solution.py:15
  83.7 7.1 %collective-permute-done = bf16[384,2,128]{2,0,1:T(8,128)(2,1)S(1)} collective-permute-done((bf16[384,2,128]{2,0,1:T(8,128)(2,1)S(1)}, bf16[384,2,128]{2,0,1:T(8,128)(2,1)S(1)}, u32[]{:S(2)}, u32[]{:S(2)}) %collective-permute-start) | collective-permute-done | bytes 196640 | tf_op jit(solution)/shard_map/while/body/eval_jaxpr/ppermute | solution.py:15
  93.1 7.1 %collective-permute-done = bf16[384,2,128]{2,0,1:T(8,128)(2,1)S(1)} collective-permute-done((bf16[384,2,128]{2,0,1:T(8,128)(2,1)S(1)}, bf16[384,2,128]{2,0,1:T(8,128)(2,1)S(1)}, u32[]{:S(2)}, u32[]{:S(2)}) %collective-permute-start) | collective-permute-done | bytes 196640 | tf_op jit(solution)/shard_map/while/body/eval_jaxpr/ppermute | solution.py:15
  102.5 7.1 %collective-permute-done = bf16[384,2,128]{2,0,1:T(8,128)(2,1)S(1)} collective-permute-done((bf16[384,2,128]{2,0,1:T(8,128)(2,1)S(1)}, bf16[384,2,128]{2,0,1:T(8,128)(2,1)S(1)}, u32[]{:S(2)}, u32[]{:S(2)}) %collective-permute-start) | collective-permute-done | bytes 196640 | tf_op jit(solution)/shard_map/while/body/eval_jaxpr/ppermute | solution.py:15
  111.9 7.1 %collective-permute-done = bf16[384,2,128]{2,0,1:T(8,128)(2,1)S(1)} collective-permute-done((bf16[384,2,128]{2,0,1:T(8,128)(2,1)S(1)}, bf16[384,2,128]{2,0,1:T(8,128)(2,1)S(1)}, u32[]{:S(2)}, u32[]{:S(2)}) %collective-permute-start) | collective-permute-done | bytes 196640 | tf_op jit(solution)/shard_map/while/body/eval_jaxpr/ppermute | solution.py:15
  120.1 1.2 convolution_add_fusion.2
  121.3 7.1 %collective-permute-done = bf16[384,2,128]{2,0,1:T(8,128)(2,1)S(1)} collective-permute-done((bf16[384,2,128]{2,0,1:T(8,128)(2,1)S(1)}, bf16[384,2,128]{2,0,1:T(8,128)(2,1)S(1)}, u32[]{:S(2)}, u32[]{:S(2)}) %collective-permute-start) | collective-permute-done | bytes 196640 | tf_op jit(solution)/shard_map/while/body/eval_jaxpr/ppermute | solution.py:15
  130.7 7.1 %collective-permute-done = bf16[384,2,128]{2,0,1:T(8,128)(2,1)S(1)} collective-permute-done((bf16[384,2,128]{2,0,1:T(8,128)(2,1)S(1)}, bf16[384,2,128]{2,0,1:T(8,128)(2,1)S(1)}, u32[]{:S(2)}, u32[]{:S(2)}) %collective-permute-start) | collective-permute-done | bytes 196640 | tf_op jit(solution)/shard_map/while/body/eval_jaxpr/ppermute | solution.py:15
  140.1 7.1 %collective-permute-done = bf16[384,2,128]{2,0,1:T(8,128)(2,1)S(1)} collective-permute-done((bf16[384,2,128]{2,0,1:T(8,128)(2,1)S(1)}, bf16[384,2,128]{2,0,1:T(8,128)(2,1)S(1)}, u32[]{:S(2)}, u32[]{:S(2)}) %collective-permute-start) | collective-permute-done | bytes 196640 | tf_op jit(solution)/shard_map/while/body/eval_jaxpr/ppermute | solution.py:15
  149.6 7.1 %collective-permute-done = bf16[384,2,128]{2,0,1:T(8,128)(2,1)S(1)} collective-permute-done((bf16[384,2,128]{2,0,1:T(8,128)(2,1)S(1)}, bf16[384,2,128]{2,0,1:T(8,128)(2,1)S(1)}, u32[]{:S(2)}, u32[]{:S(2)}) %collective-permute-start) | collective-permute-done | bytes 196640 | tf_op jit(solution)/shard_map/while/body/eval_jaxpr/ppermute | solution.py:15
  157.9 311.9 %while.39 = (s32[]{:T(128)}, f32[384,2,128]{2,0,1:T(8,128)S(1)}, bf16[384,2,128]{2,0,1:T(8,128)(2,1)S(1)}, bf16[384,2,128]{2,0,1:T(8,128)(2,1)}, f32[384,2,128]{...) while((s32[]{:T(128)}, f32[384,2,128]{2,0,1:T(8,128)S(1)}, ...), condition=%wide.region_5.6_spmd.clone, body=%wide.region_4.5_spmd.clone.sunk | while | flops 379846656 | bytes 14555423 | solution.py:95
  161.0 10.0 %collective-permute-done.2 = bf16[384,2,128]{2,0,1:T(8,128)(2,1)S(1)} collective-permute-done((bf16[384,2,128]{2,0,1:T(8,128)(2,1)S(1)}, bf16[384,2,128]{2,0,1:T(8,128)(2,1)S(1)}, u32[]{:S(2)}, u32[]{:S(2)}) %collective-permute-start.2) | collective-permute-done | bytes 196640 | tf_op jit(solution)/shard_map/while/body/eval_jaxpr/ppermute | solution.py:15
  171.0 2.1 collective-permute-done.3
  175.1 2.7 collective-permute-start.4
  178.9 11.5 %collective-permute-done.2 = bf16[384,2,128]{2,0,1:T(8,128)(2,1)S(1)} collective-permute-done((bf16[384,2,128]{2,0,1:T(8,128)(2,1)S(1)}, bf16[384,2,128]{2,0,1:T(8,128)(2,1)S(1)}, u32[]{:S(2)}, u32[]{:S(2)}) %collective-permute-start.2) | collective-permute-done | bytes 196640 | tf_op jit(solution)/shard_map/while/body/eval_jaxpr/ppermute | solution.py:15
  193.0 2.7 collective-permute-start.4
  196.7 13.6 %collective-permute-done.2 = bf16[384,2,128]{2,0,1:T(8,128)(2,1)S(1)} collective-permute-done((bf16[384,2,128]{2,0,1:T(8,128)(2,1)S(1)}, bf16[384,2,128]{2,0,1:T(8,128)(2,1)S(1)}, u32[]{:S(2)}, u32[]{:S(2)}) %collective-permute-start.2) | collective-permute-done | bytes 196640 | tf_op jit(solution)/shard_map/while/body/eval_jaxpr/ppermute | solution.py:15
  214.6 15.7 %collective-permute-done.2 = bf16[384,2,128]{2,0,1:T(8,128)(2,1)S(1)} collective-permute-done((bf16[384,2,128]{2,0,1:T(8,128)(2,1)S(1)}, bf16[384,2,128]{2,0,1:T(8,128)(2,1)S(1)}, u32[]{:S(2)}, u32[]{:S(2)}) %collective-permute-start.2) | collective-permute-done | bytes 196640 | tf_op jit(solution)/shard_map/while/body/eval_jaxpr/ppermute | solution.py:15
  233.6 16.6 %collective-permute-done.2 = bf16[384,2,128]{2,0,1:T(8,128)(2,1)S(1)} collective-permute-done((bf16[384,2,128]{2,0,1:T(8,128)(2,1)S(1)}, bf16[384,2,128]{2,0,1:T(8,128)(2,1)S(1)}, u32[]{:S(2)}, u32[]{:S(2)}) %collective-permute-start.2) | collective-permute-done | bytes 196640 | tf_op jit(solution)/shard_map/while/body/eval_jaxpr/ppermute | solution.py:15
  253.5 16.6 %collective-permute-done.2 = bf16[384,2,128]{2,0,1:T(8,128)(2,1)S(1)} collective-permute-done((bf16[384,2,128]{2,0,1:T(8,128)(2,1)S(1)}, bf16[384,2,128]{2,0,1:T(8,128)(2,1)S(1)}, u32[]{:S(2)}, u32[]{:S(2)}) %collective-permute-start.2) | collective-permute-done | bytes 196640 | tf_op jit(solution)/shard_map/while/body/eval_jaxpr/ppermute | solution.py:15
  273.5 16.6 %collective-permute-done.2 = bf16[384,2,128]{2,0,1:T(8,128)(2,1)S(1)} collective-permute-done((bf16[384,2,128]{2,0,1:T(8,128)(2,1)S(1)}, bf16[384,2,128]{2,0,1:T(8,128)(2,1)S(1)}, u32[]{:S(2)}, u32[]{:S(2)}) %collective-permute-start.2) | collective-permute-done | bytes 196640 | tf_op jit(solution)/shard_map/while/body/eval_jaxpr/ppermute | solution.py:15
  293.4 16.6 %collective-permute-done.2 = bf16[384,2,128]{2,0,1:T(8,128)(2,1)S(1)} collective-permute-done((bf16[384,2,128]{2,0,1:T(8,128)(2,1)S(1)}, bf16[384,2,128]{2,0,1:T(8,128)(2,1)S(1)}, u32[]{:S(2)}, u32[]{:S(2)}) %collective-permute-start.2) | collective-permute-done | bytes 196640 | tf_op jit(solution)/shard_map/while/body/eval_jaxpr/ppermute | solution.py:15
  313.4 16.6 %collective-permute-done.2 = bf16[384,2,128]{2,0,1:T(8,128)(2,1)S(1)} collective-permute-done((bf16[384,2,128]{2,0,1:T(8,128)(2,1)S(1)}, bf16[384,2,128]{2,0,1:T(8,128)(2,1)S(1)}, u32[]{:S(2)}, u32[]{:S(2)}) %collective-permute-start.2) | collective-permute-done | bytes 196640 | tf_op jit(solution)/shard_map/while/body/eval_jaxpr/ppermute | solution.py:15
  333.3 16.6 %collective-permute-done.2 = bf16[384,2,128]{2,0,1:T(8,128)(2,1)S(1)} collective-permute-done((bf16[384,2,128]{2,0,1:T(8,128)(2,1)S(1)}, bf16[384,2,128]{2,0,1:T(8,128)(2,1)S(1)}, u32[]{:S(2)}, u32[]{:S(2)}) %collective-permute-start.2) | collective-permute-done | bytes 196640 | tf_op jit(solution)/shard_map/while/body/eval_jaxpr/ppermute | solution.py:15
  353.3 16.6 %collective-permute-done.2 = bf16[384,2,128]{2,0,1:T(8,128)(2,1)S(1)} collective-permute-done((bf16[384,2,128]{2,0,1:T(8,128)(2,1)S(1)}, bf16[384,2,128]{2,0,1:T(8,128)(2,1)S(1)}, u32[]{:S(2)}, u32[]{:S(2)}) %collective-permute-start.2) | collective-permute-done | bytes 196640 | tf_op jit(solution)/shard_map/while/body/eval_jaxpr/ppermute | solution.py:15
  373.2 16.6 %collective-permute-done.2 = bf16[384,2,128]{2,0,1:T(8,128)(2,1)S(1)} collective-permute-done((bf16[384,2,128]{2,0,1:T(8,128)(2,1)S(1)}, bf16[384,2,128]{2,0,1:T(8,128)(2,1)S(1)}, u32[]{:S(2)}, u32[]{:S(2)}) %collective-permute-start.2) | collective-permute-done | bytes 196640 | tf_op jit(solution)/shard_map/while/body/eval_jaxpr/ppermute | solution.py:15
  393.2 16.6 %collective-permute-done.2 = bf16[384,2,128]{2,0,1:T(8,128)(2,1)S(1)} collective-permute-done((bf16[384,2,128]{2,0,1:T(8,128)(2,1)S(1)}, bf16[384,2,128]{2,0,1:T(8,128)(2,1)S(1)}, u32[]{:S(2)}, u32[]{:S(2)}) %collective-permute-start.2) | collective-permute-done | bytes 196640 | tf_op jit(solution)/shard_map/while/body/eval_jaxpr/ppermute | solution.py:15
  413.1 16.6 %collective-permute-done.2 = bf16[384,2,128]{2,0,1:T(8,128)(2,1)S(1)} collective-permute-done((bf16[384,2,128]{2,0,1:T(8,128)(2,1)S(1)}, bf16[384,2,128]{2,0,1:T(8,128)(2,1)S(1)}, u32[]{:S(2)}, u32[]{:S(2)}) %collective-permute-start.2) | collective-permute-done | bytes 196640 | tf_op jit(solution)/shard_map/while/body/eval_jaxpr/ppermute | solution.py:15
  433.1 16.6 %collective-permute-done.2 = bf16[384,2,128]{2,0,1:T(8,128)(2,1)S(1)} collective-permute-done((bf16[384,2,128]{2,0,1:T(8,128)(2,1)S(1)}, bf16[384,2,128]{2,0,1:T(8,128)(2,1)S(1)}, u32[]{:S(2)}, u32[]{:S(2)}) %collective-permute-start.2) | collective-permute-done | bytes 196640 | tf_op jit(solution)/shard_map/while/body/eval_jaxpr/ppermute | solution.py:15
  453.0 16.6 %collective-permute-done.2 = bf16[384,2,128]{2,0,1:T(8,128)(2,1)S(1)} collective-permute-done((bf16[384,2,128]{2,0,1:T(8,128)(2,1)S(1)}, bf16[384,2,128]{2,0,1:T(8,128)(2,1)S(1)}, u32[]{:S(2)}, u32[]{:S(2)}) %collective-permute-start.2) | collective-permute-done | bytes 196640 | tf_op jit(solution)/shard_map/while/body/eval_jaxpr/ppermute | solution.py:15
  470.9 5.8 %bitcast_convert_fusion = bf16[384,3072]{1,0:T(8,128)(2,1)} fusion(bf16[3,3072,256]{2,1,0:T(8,128)(2,1)} %param.13, bf16[1,384,256]{2,1,0:T(8,128)(2,1)S(1)} %stack.14, bf16[1,384,256]{2,1,0:T(8,128)(2,1)S(1)} %stack.13, bf16[1,384,256]{2,1,0:T(8,128)(2,1)S(1)} %stack.12), kind=kOutput, calls=%fused_computation.26 | convolution fusion | flops 1813708800 | bytes 7667712 | tf_op jit(solution)/shard_map/tqc,tdc->qd/dot_general | solution.py:102
  476.8 52.3 %reduce-scatter.3.cloned.1.call-done = bf16[48,3072]{1,0:T(8,128)(2,1)} async-done(((bf16[384,3072]{1,0:T(8,128)(2,1)}), bf16[48,3072]{1,0:T(8,128)(2,1)}) %reduce-scatter.3.cloned.1.call-update) | async-done | bytes 294928 | tf_op jit(solution)/shard_map/reduce_scatter | solution.py:101
  529.1 24.5 %reduce-scatter.5.cloned.1.call-done = bf16[48,1536]{1,0:T(8,128)(2,1)} async-done(((bf16[48,3072]{1,0:T(8,128)(2,1)}), bf16[48,1536]{1,0:T(8,128)(2,1)}) %reduce-scatter.5.cloned.1.call-update) | async-done | bytes 147472 | tf_op jit(solution)/shard_map/reduce_scatter | solution.py:109
  (433 shorter events, 93.1 us)
Async XLA Ops:
  6.5 522.6 %reduce-scatter.3.cloned.1.call-start = ((), (), s32[]{:S(2)}) async-start(), calls=%async_computation.2 | async-start | bytes 2654208 | tf_op jit(solution)/shard_map/reduce_scatter | solution.py:101
  193.0 17.4 %collective-permute-start.4 = (f32[384,2,128]{2,0,1:T(8,128)S(1)}, f32[384,2,128]{2,0,1:T(8,128)S(1)}, u32[]{:S(2)}, u32[]{:S(2)}) collective-permute-start(f32[384,2,128]{2,0,1:T(8,128)S(1)} %fusion.76), channel_id=1, source_target_pairs={{0,8},{8,16},{16,24},{24,32},{32,40},{40,48},{48,56},{56,64},{64,7... | collective-permute-start | bytes 1179656 | tf_op jit(solution)/shard_map/while/body/eval_jaxpr/ppermute | solution.py:15
  212.5 17.9 %collective-permute-start.4 = (f32[384,2,128]{2,0,1:T(8,128)S(1)}, f32[384,2,128]{2,0,1:T(8,128)S(1)}, u32[]{:S(2)}, u32[]{:S(2)}) collective-permute-start(f32[384,2,128]{2,0,1:T(8,128)S(1)} %fusion.76), channel_id=1, source_target_pairs={{0,8},{8,16},{16,24},{24,32},{32,40},{40,48},{48,56},{56,64},{64,7... | collective-permute-start | bytes 1179656 | tf_op jit(solution)/shard_map/while/body/eval_jaxpr/ppermute | solution.py:15
  232.4 17.9 %collective-permute-start.4 = (f32[384,2,128]{2,0,1:T(8,128)S(1)}, f32[384,2,128]{2,0,1:T(8,128)S(1)}, u32[]{:S(2)}, u32[]{:S(2)}) collective-permute-start(f32[384,2,128]{2,0,1:T(8,128)S(1)} %fusion.76), channel_id=1, source_target_pairs={{0,8},{8,16},{16,24},{24,32},{32,40},{40,48},{48,56},{56,64},{64,7... | collective-permute-start | bytes 1179656 | tf_op jit(solution)/shard_map/while/body/eval_jaxpr/ppermute | solution.py:15
  232.9 17.5 %collective-permute-start.5 = (f32[384,2,128]{2,0,1:T(8,128)S(1)}, f32[384,2,128]{2,0,1:T(8,128)S(1)}, u32[]{:S(2)}, u32[]{:S(2)}) collective-permute-start(f32[384,2,128]{2,0,1:T(8,128)S(1)} %fusion.77), channel_id=1, source_target_pairs={{0,8},{8,16},{16,24},{24,32},{32,40},{40,48},{48,56},{56,64},{64,7... | collective-permute-start | bytes 1179656 | tf_op jit(solution)/shard_map/while/body/eval_jaxpr/ppermute | solution.py:15
  233.0 17.2 %collective-permute-start.2 = (bf16[384,2,128]{2,0,1:T(8,128)(2,1)S(1)}, bf16[384,2,128]{2,0,1:T(8,128)(2,1)S(1)}, u32[]{:S(2)}, u32[]{:S(2)}) collective-permute-start(bf16[384,2,128]{2,0,1:T(8,128)(2,1)S(1)} %copy.63), channel_id=1, source_target_pairs={{0,8},{8,16},{16,24},{24,32},{32,40},{40,48},{48,56},{56,64},{64,7... | collective-permute-start | bytes 589832 | tf_op jit(solution)/shard_map/while/body/eval_jaxpr/ppermute | solution.py:15
  233.1 17.3 %collective-permute-start.3 = (bf16[384,2,128]{2,0,1:T(8,128)(2,1)S(1)}, bf16[384,2,128]{2,0,1:T(8,128)(2,1)}, u32[]{:S(2)}, u32[]{:S(2)}) collective-permute-start(bf16[384,2,128]{2,0,1:T(8,128)(2,1)S(1)} %copy.64), channel_id=1, source_target_pairs={{0,8},{8,16},{16,24},{24,32},{32,40},{40,48},{48,56},{56,64},{64,7... | collective-permute-start | bytes 589832 | tf_op jit(solution)/shard_map/while/body/eval_jaxpr/ppermute | solution.py:15
  252.4 17.9 %collective-permute-start.4 = (f32[384,2,128]{2,0,1:T(8,128)S(1)}, f32[384,2,128]{2,0,1:T(8,128)S(1)}, u32[]{:S(2)}, u32[]{:S(2)}) collective-permute-start(f32[384,2,128]{2,0,1:T(8,128)S(1)} %fusion.76), channel_id=1, source_target_pairs={{0,8},{8,16},{16,24},{24,32},{32,40},{40,48},{48,56},{56,64},{64,7... | collective-permute-start | bytes 1179656 | tf_op jit(solution)/shard_map/while/body/eval_jaxpr/ppermute | solution.py:15
  252.8 17.5 %collective-permute-start.5 = (f32[384,2,128]{2,0,1:T(8,128)S(1)}, f32[384,2,128]{2,0,1:T(8,128)S(1)}, u32[]{:S(2)}, u32[]{:S(2)}) collective-permute-start(f32[384,2,128]{2,0,1:T(8,128)S(1)} %fusion.77), channel_id=1, source_target_pairs={{0,8},{8,16},{16,24},{24,32},{32,40},{40,48},{48,56},{56,64},{64,7... | collective-permute-start | bytes 1179656 | tf_op jit(solution)/shard_map/while/body/eval_jaxpr/ppermute | solution.py:15
  252.9 17.2 %collective-permute-start.2 = (bf16[384,2,128]{2,0,1:T(8,128)(2,1)S(1)}, bf16[384,2,128]{2,0,1:T(8,128)(2,1)S(1)}, u32[]{:S(2)}, u32[]{:S(2)}) collective-permute-start(bf16[384,2,128]{2,0,1:T(8,128)(2,1)S(1)} %copy.63), channel_id=1, source_target_pairs={{0,8},{8,16},{16,24},{24,32},{32,40},{40,48},{48,56},{56,64},{64,7... | collective-permute-start | bytes 589832 | tf_op jit(solution)/shard_map/while/body/eval_jaxpr/ppermute | solution.py:15
  253.0 17.3 %collective-permute-start.3 = (bf16[384,2,128]{2,0,1:T(8,128)(2,1)S(1)}, bf16[384,2,128]{2,0,1:T(8,128)(2,1)}, u32[]{:S(2)}, u32[]{:S(2)}) collective-permute-start(bf16[384,2,128]{2,0,1:T(8,128)(2,1)S(1)} %copy.64), channel_id=1, source_target_pairs={{0,8},{8,16},{16,24},{24,32},{32,40},{40,48},{48,56},{56,64},{64,7... | collective-permute-start | bytes 589832 | tf_op jit(solution)/shard_map/while/body/eval_jaxpr/ppermute | solution.py:15
  272.3 17.9 %collective-permute-start.4 = (f32[384,2,128]{2,0,1:T(8,128)S(1)}, f32[384,2,128]{2,0,1:T(8,128)S(1)}, u32[]{:S(2)}, u32[]{:S(2)}) collective-permute-start(f32[384,2,128]{2,0,1:T(8,128)S(1)} %fusion.76), channel_id=1, source_target_pairs={{0,8},{8,16},{16,24},{24,32},{32,40},{40,48},{48,56},{56,64},{64,7... | collective-permute-start | bytes 1179656 | tf_op jit(solution)/shard_map/while/body/eval_jaxpr/ppermute | solution.py:15
  272.8 17.5 %collective-permute-start.5 = (f32[384,2,128]{2,0,1:T(8,128)S(1)}, f32[384,2,128]{2,0,1:T(8,128)S(1)}, u32[]{:S(2)}, u32[]{:S(2)}) collective-permute-start(f32[384,2,128]{2,0,1:T(8,128)S(1)} %fusion.77), channel_id=1, source_target_pairs={{0,8},{8,16},{16,24},{24,32},{32,40},{40,48},{48,56},{56,64},{64,7... | collective-permute-start | bytes 1179656 | tf_op jit(solution)/shard_map/while/body/eval_jaxpr/ppermute | solution.py:15
  272.9 17.2 %collective-permute-start.2 = (bf16[384,2,128]{2,0,1:T(8,128)(2,1)S(1)}, bf16[384,2,128]{2,0,1:T(8,128)(2,1)S(1)}, u32[]{:S(2)}, u32[]{:S(2)}) collective-permute-start(bf16[384,2,128]{2,0,1:T(8,128)(2,1)S(1)} %copy.63), channel_id=1, source_target_pairs={{0,8},{8,16},{16,24},{24,32},{32,40},{40,48},{48,56},{56,64},{64,7... | collective-permute-start | bytes 589832 | tf_op jit(solution)/shard_map/while/body/eval_jaxpr/ppermute | solution.py:15
  273.0 17.3 %collective-permute-start.3 = (bf16[384,2,128]{2,0,1:T(8,128)(2,1)S(1)}, bf16[384,2,128]{2,0,1:T(8,128)(2,1)}, u32[]{:S(2)}, u32[]{:S(2)}) collective-permute-start(bf16[384,2,128]{2,0,1:T(8,128)(2,1)S(1)} %copy.64), channel_id=1, source_target_pairs={{0,8},{8,16},{16,24},{24,32},{32,40},{40,48},{48,56},{56,64},{64,7... | collective-permute-start | bytes 589832 | tf_op jit(solution)/shard_map/while/body/eval_jaxpr/ppermute | solution.py:15
  292.3 17.9 %collective-permute-start.4 = (f32[384,2,128]{2,0,1:T(8,128)S(1)}, f32[384,2,128]{2,0,1:T(8,128)S(1)}, u32[]{:S(2)}, u32[]{:S(2)}) collective-permute-start(f32[384,2,128]{2,0,1:T(8,128)S(1)} %fusion.76), channel_id=1, source_target_pairs={{0,8},{8,16},{16,24},{24,32},{32,40},{40,48},{48,56},{56,64},{64,7... | collective-permute-start | bytes 1179656 | tf_op jit(solution)/shard_map/while/body/eval_jaxpr/ppermute | solution.py:15
  292.7 17.5 %collective-permute-start.5 = (f32[384,2,128]{2,0,1:T(8,128)S(1)}, f32[384,2,128]{2,0,1:T(8,128)S(1)}, u32[]{:S(2)}, u32[]{:S(2)}) collective-permute-start(f32[384,2,128]{2,0,1:T(8,128)S(1)} %fusion.77), channel_id=1, source_target_pairs={{0,8},{8,16},{16,24},{24,32},{32,40},{40,48},{48,56},{56,64},{64,7... | collective-permute-start | bytes 1179656 | tf_op jit(solution)/shard_map/while/body/eval_jaxpr/ppermute | solution.py:15
  292.8 17.2 %collective-permute-start.2 = (bf16[384,2,128]{2,0,1:T(8,128)(2,1)S(1)}, bf16[384,2,128]{2,0,1:T(8,128)(2,1)S(1)}, u32[]{:S(2)}, u32[]{:S(2)}) collective-permute-start(bf16[384,2,128]{2,0,1:T(8,128)(2,1)S(1)} %copy.63), channel_id=1, source_target_pairs={{0,8},{8,16},{16,24},{24,32},{32,40},{40,48},{48,56},{56,64},{64,7... | collective-permute-start | bytes 589832 | tf_op jit(solution)/shard_map/while/body/eval_jaxpr/ppermute | solution.py:15
  292.9 17.3 %collective-permute-start.3 = (bf16[384,2,128]{2,0,1:T(8,128)(2,1)S(1)}, bf16[384,2,128]{2,0,1:T(8,128)(2,1)}, u32[]{:S(2)}, u32[]{:S(2)}) collective-permute-start(bf16[384,2,128]{2,0,1:T(8,128)(2,1)S(1)} %copy.64), channel_id=1, source_target_pairs={{0,8},{8,16},{16,24},{24,32},{32,40},{40,48},{48,56},{56,64},{64,7... | collective-permute-start | bytes 589832 | tf_op jit(solution)/shard_map/while/body/eval_jaxpr/ppermute | solution.py:15
  312.2 17.9 %collective-permute-start.4 = (f32[384,2,128]{2,0,1:T(8,128)S(1)}, f32[384,2,128]{2,0,1:T(8,128)S(1)}, u32[]{:S(2)}, u32[]{:S(2)}) collective-permute-start(f32[384,2,128]{2,0,1:T(8,128)S(1)} %fusion.76), channel_id=1, source_target_pairs={{0,8},{8,16},{16,24},{24,32},{32,40},{40,48},{48,56},{56,64},{64,7... | collective-permute-start | bytes 1179656 | tf_op jit(solution)/shard_map/while/body/eval_jaxpr/ppermute | solution.py:15
  312.7 17.5 %collective-permute-start.5 = (f32[384,2,128]{2,0,1:T(8,128)S(1)}, f32[384,2,128]{2,0,1:T(8,128)S(1)}, u32[]{:S(2)}, u32[]{:S(2)}) collective-permute-start(f32[384,2,128]{2,0,1:T(8,128)S(1)} %fusion.77), channel_id=1, source_target_pairs={{0,8},{8,16},{16,24},{24,32},{32,40},{40,48},{48,56},{56,64},{64,7... | collective-permute-start | bytes 1179656 | tf_op jit(solution)/shard_map/while/body/eval_jaxpr/ppermute | solution.py:15
  312.9 17.3 %collective-permute-start.3 = (bf16[384,2,128]{2,0,1:T(8,128)(2,1)S(1)}, bf16[384,2,128]{2,0,1:T(8,128)(2,1)}, u32[]{:S(2)}, u32[]{:S(2)}) collective-permute-start(bf16[384,2,128]{2,0,1:T(8,128)(2,1)S(1)} %copy.64), channel_id=1, source_target_pairs={{0,8},{8,16},{16,24},{24,32},{32,40},{40,48},{48,56},{56,64},{64,7... | collective-permute-start | bytes 589832 | tf_op jit(solution)/shard_map/while/body/eval_jaxpr/ppermute | solution.py:15
  332.2 17.9 %collective-permute-start.4 = (f32[384,2,128]{2,0,1:T(8,128)S(1)}, f32[384,2,128]{2,0,1:T(8,128)S(1)}, u32[]{:S(2)}, u32[]{:S(2)}) collective-permute-start(f32[384,2,128]{2,0,1:T(8,128)S(1)} %fusion.76), channel_id=1, source_target_pairs={{0,8},{8,16},{16,24},{24,32},{32,40},{40,48},{48,56},{56,64},{64,7... | collective-permute-start | bytes 1179656 | tf_op jit(solution)/shard_map/while/body/eval_jaxpr/ppermute | solution.py:15
  332.6 17.5 %collective-permute-start.5 = (f32[384,2,128]{2,0,1:T(8,128)S(1)}, f32[384,2,128]{2,0,1:T(8,128)S(1)}, u32[]{:S(2)}, u32[]{:S(2)}) collective-permute-start(f32[384,2,128]{2,0,1:T(8,128)S(1)} %fusion.77), channel_id=1, source_target_pairs={{0,8},{8,16},{16,24},{24,32},{32,40},{40,48},{48,56},{56,64},{64,7... | collective-permute-start | bytes 1179656 | tf_op jit(solution)/shard_map/while/body/eval_jaxpr/ppermute | solution.py:15
  332.7 17.2 %collective-permute-start.2 = (bf16[384,2,128]{2,0,1:T(8,128)(2,1)S(1)}, bf16[384,2,128]{2,0,1:T(8,128)(2,1)S(1)}, u32[]{:S(2)}, u32[]{:S(2)}) collective-permute-start(bf16[384,2,128]{2,0,1:T(8,128)(2,1)S(1)} %copy.63), channel_id=1, source_target_pairs={{0,8},{8,16},{16,24},{24,32},{32,40},{40,48},{48,56},{56,64},{64,7... | collective-permute-start | bytes 589832 | tf_op jit(solution)/shard_map/while/body/eval_jaxpr/ppermute | solution.py:15
  332.8 17.3 %collective-permute-start.3 = (bf16[384,2,128]{2,0,1:T(8,128)(2,1)S(1)}, bf16[384,2,128]{2,0,1:T(8,128)(2,1)}, u32[]{:S(2)}, u32[]{:S(2)}) collective-permute-start(bf16[384,2,128]{2,0,1:T(8,128)(2,1)S(1)} %copy.64), channel_id=1, source_target_pairs={{0,8},{8,16},{16,24},{24,32},{32,40},{40,48},{48,56},{56,64},{64,7... | collective-permute-start | bytes 589832 | tf_op jit(solution)/shard_map/while/body/eval_jaxpr/ppermute | solution.py:15
  352.1 17.9 %collective-permute-start.4 = (f32[384,2,128]{2,0,1:T(8,128)S(1)}, f32[384,2,128]{2,0,1:T(8,128)S(1)}, u32[]{:S(2)}, u32[]{:S(2)}) collective-permute-start(f32[384,2,128]{2,0,1:T(8,128)S(1)} %fusion.76), channel_id=1, source_target_pairs={{0,8},{8,16},{16,24},{24,32},{32,40},{40,48},{48,56},{56,64},{64,7... | collective-permute-start | bytes 1179656 | tf_op jit(solution)/shard_map/while/body/eval_jaxpr/ppermute | solution.py:15
  352.6 17.5 %collective-permute-start.5 = (f32[384,2,128]{2,0,1:T(8,128)S(1)}, f32[384,2,128]{2,0,1:T(8,128)S(1)}, u32[]{:S(2)}, u32[]{:S(2)}) collective-permute-start(f32[384,2,128]{2,0,1:T(8,128)S(1)} %fusion.77), channel_id=1, source_target_pairs={{0,8},{8,16},{16,24},{24,32},{32,40},{40,48},{48,56},{56,64},{64,7... | collective-permute-start | bytes 1179656 | tf_op jit(solution)/shard_map/while/body/eval_jaxpr/ppermute | solution.py:15
  352.8 17.3 %collective-permute-start.3 = (bf16[384,2,128]{2,0,1:T(8,128)(2,1)S(1)}, bf16[384,2,128]{2,0,1:T(8,128)(2,1)}, u32[]{:S(2)}, u32[]{:S(2)}) collective-permute-start(bf16[384,2,128]{2,0,1:T(8,128)(2,1)S(1)} %copy.64), channel_id=1, source_target_pairs={{0,8},{8,16},{16,24},{24,32},{32,40},{40,48},{48,56},{56,64},{64,7... | collective-permute-start | bytes 589832 | tf_op jit(solution)/shard_map/while/body/eval_jaxpr/ppermute | solution.py:15
  372.1 17.9 %collective-permute-start.4 = (f32[384,2,128]{2,0,1:T(8,128)S(1)}, f32[384,2,128]{2,0,1:T(8,128)S(1)}, u32[]{:S(2)}, u32[]{:S(2)}) collective-permute-start(f32[384,2,128]{2,0,1:T(8,128)S(1)} %fusion.76), channel_id=1, source_target_pairs={{0,8},{8,16},{16,24},{24,32},{32,40},{40,48},{48,56},{56,64},{64,7... | collective-permute-start | bytes 1179656 | tf_op jit(solution)/shard_map/while/body/eval_jaxpr/ppermute | solution.py:15
  372.5 17.5 %collective-permute-start.5 = (f32[384,2,128]{2,0,1:T(8,128)S(1)}, f32[384,2,128]{2,0,1:T(8,128)S(1)}, u32[]{:S(2)}, u32[]{:S(2)}) collective-permute-start(f32[384,2,128]{2,0,1:T(8,128)S(1)} %fusion.77), channel_id=1, source_target_pairs={{0,8},{8,16},{16,24},{24,32},{32,40},{40,48},{48,56},{56,64},{64,7... | collective-permute-start | bytes 1179656 | tf_op jit(solution)/shard_map/while/body/eval_jaxpr/ppermute | solution.py:15
  372.7 17.3 %collective-permute-start.3 = (bf16[384,2,128]{2,0,1:T(8,128)(2,1)S(1)}, bf16[384,2,128]{2,0,1:T(8,128)(2,1)}, u32[]{:S(2)}, u32[]{:S(2)}) collective-permute-start(bf16[384,2,128]{2,0,1:T(8,128)(2,1)S(1)} %copy.64), channel_id=1, source_target_pairs={{0,8},{8,16},{16,24},{24,32},{32,40},{40,48},{48,56},{56,64},{64,7... | collective-permute-start | bytes 589832 | tf_op jit(solution)/shard_map/while/body/eval_jaxpr/ppermute | solution.py:15
  392.0 17.9 %collective-permute-start.4 = (f32[384,2,128]{2,0,1:T(8,128)S(1)}, f32[384,2,128]{2,0,1:T(8,128)S(1)}, u32[]{:S(2)}, u32[]{:S(2)}) collective-permute-start(f32[384,2,128]{2,0,1:T(8,128)S(1)} %fusion.76), channel_id=1, source_target_pairs={{0,8},{8,16},{16,24},{24,32},{32,40},{40,48},{48,56},{56,64},{64,7... | collective-permute-start | bytes 1179656 | tf_op jit(solution)/shard_map/while/body/eval_jaxpr/ppermute | solution.py:15
  392.5 17.5 %collective-permute-start.5 = (f32[384,2,128]{2,0,1:T(8,128)S(1)}, f32[384,2,128]{2,0,1:T(8,128)S(1)}, u32[]{:S(2)}, u32[]{:S(2)}) collective-permute-start(f32[384,2,128]{2,0,1:T(8,128)S(1)} %fusion.77), channel_id=1, source_target_pairs={{0,8},{8,16},{16,24},{24,32},{32,40},{40,48},{48,56},{56,64},{64,7... | collective-permute-start | bytes 1179656 | tf_op jit(solution)/shard_map/while/body/eval_jaxpr/ppermute | solution.py:15
  392.6 17.2 %collective-permute-start.2 = (bf16[384,2,128]{2,0,1:T(8,128)(2,1)S(1)}, bf16[384,2,128]{2,0,1:T(8,128)(2,1)S(1)}, u32[]{:S(2)}, u32[]{:S(2)}) collective-permute-start(bf16[384,2,128]{2,0,1:T(8,128)(2,1)S(1)} %copy.63), channel_id=1, source_target_pairs={{0,8},{8,16},{16,24},{24,32},{32,40},{40,48},{48,56},{56,64},{64,7... | collective-permute-start | bytes 589832 | tf_op jit(solution)/shard_map/while/body/eval_jaxpr/ppermute | solution.py:15
  392.7 17.3 %collective-permute-start.3 = (bf16[384,2,128]{2,0,1:T(8,128)(2,1)S(1)}, bf16[384,2,128]{2,0,1:T(8,128)(2,1)}, u32[]{:S(2)}, u32[]{:S(2)}) collective-permute-start(bf16[384,2,128]{2,0,1:T(8,128)(2,1)S(1)} %copy.64), channel_id=1, source_target_pairs={{0,8},{8,16},{16,24},{24,32},{32,40},{40,48},{48,56},{56,64},{64,7... | collective-permute-start | bytes 589832 | tf_op jit(solution)/shard_map/while/body/eval_jaxpr/ppermute | solution.py:15
  412.0 17.9 %collective-permute-start.4 = (f32[384,2,128]{2,0,1:T(8,128)S(1)}, f32[384,2,128]{2,0,1:T(8,128)S(1)}, u32[]{:S(2)}, u32[]{:S(2)}) collective-permute-start(f32[384,2,128]{2,0,1:T(8,128)S(1)} %fusion.76), channel_id=1, source_target_pairs={{0,8},{8,16},{16,24},{24,32},{32,40},{40,48},{48,56},{56,64},{64,7... | collective-permute-start | bytes 1179656 | tf_op jit(solution)/shard_map/while/body/eval_jaxpr/ppermute | solution.py:15
  412.4 17.5 %collective-permute-start.5 = (f32[384,2,128]{2,0,1:T(8,128)S(1)}, f32[384,2,128]{2,0,1:T(8,128)S(1)}, u32[]{:S(2)}, u32[]{:S(2)}) collective-permute-start(f32[384,2,128]{2,0,1:T(8,128)S(1)} %fusion.77), channel_id=1, source_target_pairs={{0,8},{8,16},{16,24},{24,32},{32,40},{40,48},{48,56},{56,64},{64,7... | collective-permute-start | bytes 1179656 | tf_op jit(solution)/shard_map/while/body/eval_jaxpr/ppermute | solution.py:15
  412.5 17.2 %collective-permute-start.2 = (bf16[384,2,128]{2,0,1:T(8,128)(2,1)S(1)}, bf16[384,2,128]{2,0,1:T(8,128)(2,1)S(1)}, u32[]{:S(2)}, u32[]{:S(2)}) collective-permute-start(bf16[384,2,128]{2,0,1:T(8,128)(2,1)S(1)} %copy.63), channel_id=1, source_target_pairs={{0,8},{8,16},{16,24},{24,32},{32,40},{40,48},{48,56},{56,64},{64,7... | collective-permute-start | bytes 589832 | tf_op jit(solution)/shard_map/while/body/eval_jaxpr/ppermute | solution.py:15
  412.6 17.3 %collective-permute-start.3 = (bf16[384,2,128]{2,0,1:T(8,128)(2,1)S(1)}, bf16[384,2,128]{2,0,1:T(8,128)(2,1)}, u32[]{:S(2)}, u32[]{:S(2)}) collective-permute-start(bf16[384,2,128]{2,0,1:T(8,128)(2,1)S(1)} %copy.64), channel_id=1, source_target_pairs={{0,8},{8,16},{16,24},{24,32},{32,40},{40,48},{48,56},{56,64},{64,7... | collective-permute-start | bytes 589832 | tf_op jit(solution)/shard_map/while/body/eval_jaxpr/ppermute | solution.py:15
  431.9 17.9 %collective-permute-start.4 = (f32[384,2,128]{2,0,1:T(8,128)S(1)}, f32[384,2,128]{2,0,1:T(8,128)S(1)}, u32[]{:S(2)}, u32[]{:S(2)}) collective-permute-start(f32[384,2,128]{2,0,1:T(8,128)S(1)} %fusion.76), channel_id=1, source_target_pairs={{0,8},{8,16},{16,24},{24,32},{32,40},{40,48},{48,56},{56,64},{64,7... | collective-permute-start | bytes 1179656 | tf_op jit(solution)/shard_map/while/body/eval_jaxpr/ppermute | solution.py:15
  432.4 17.5 %collective-permute-start.5 = (f32[384,2,128]{2,0,1:T(8,128)S(1)}, f32[384,2,128]{2,0,1:T(8,128)S(1)}, u32[]{:S(2)}, u32[]{:S(2)}) collective-permute-start(f32[384,2,128]{2,0,1:T(8,128)S(1)} %fusion.77), channel_id=1, source_target_pairs={{0,8},{8,16},{16,24},{24,32},{32,40},{40,48},{48,56},{56,64},{64,7... | collective-permute-start | bytes 1179656 | tf_op jit(solution)/shard_map/while/body/eval_jaxpr/ppermute | solution.py:15
  432.6 17.3 %collective-permute-start.3 = (bf16[384,2,128]{2,0,1:T(8,128)(2,1)S(1)}, bf16[384,2,128]{2,0,1:T(8,128)(2,1)}, u32[]{:S(2)}, u32[]{:S(2)}) collective-permute-start(bf16[384,2,128]{2,0,1:T(8,128)(2,1)S(1)} %copy.64), channel_id=1, source_target_pairs={{0,8},{8,16},{16,24},{24,32},{32,40},{40,48},{48,56},{56,64},{64,7... | collective-permute-start | bytes 589832 | tf_op jit(solution)/shard_map/while/body/eval_jaxpr/ppermute | solution.py:15
  451.9 17.9 %collective-permute-start.4 = (f32[384,2,128]{2,0,1:T(8,128)S(1)}, f32[384,2,128]{2,0,1:T(8,128)S(1)}, u32[]{:S(2)}, u32[]{:S(2)}) collective-permute-start(f32[384,2,128]{2,0,1:T(8,128)S(1)} %fusion.76), channel_id=1, source_target_pairs={{0,8},{8,16},{16,24},{24,32},{32,40},{40,48},{48,56},{56,64},{64,7... | collective-permute-start | bytes 1179656 | tf_op jit(solution)/shard_map/while/body/eval_jaxpr/ppermute | solution.py:15
  452.3 17.5 %collective-permute-start.5 = (f32[384,2,128]{2,0,1:T(8,128)S(1)}, f32[384,2,128]{2,0,1:T(8,128)S(1)}, u32[]{:S(2)}, u32[]{:S(2)}) collective-permute-start(f32[384,2,128]{2,0,1:T(8,128)S(1)} %fusion.77), channel_id=1, source_target_pairs={{0,8},{8,16},{16,24},{24,32},{32,40},{40,48},{48,56},{56,64},{64,7... | collective-permute-start | bytes 1179656 | tf_op jit(solution)/shard_map/while/body/eval_jaxpr/ppermute | solution.py:15
  452.4 17.2 %collective-permute-start.2 = (bf16[384,2,128]{2,0,1:T(8,128)(2,1)S(1)}, bf16[384,2,128]{2,0,1:T(8,128)(2,1)S(1)}, u32[]{:S(2)}, u32[]{:S(2)}) collective-permute-start(bf16[384,2,128]{2,0,1:T(8,128)(2,1)S(1)} %copy.63), channel_id=1, source_target_pairs={{0,8},{8,16},{16,24},{24,32},{32,40},{40,48},{48,56},{56,64},{64,7... | collective-permute-start | bytes 589832 | tf_op jit(solution)/shard_map/while/body/eval_jaxpr/ppermute | solution.py:15
  452.5 17.3 %collective-permute-start.3 = (bf16[384,2,128]{2,0,1:T(8,128)(2,1)S(1)}, bf16[384,2,128]{2,0,1:T(8,128)(2,1)}, u32[]{:S(2)}, u32[]{:S(2)}) collective-permute-start(bf16[384,2,128]{2,0,1:T(8,128)(2,1)S(1)} %copy.64), channel_id=1, source_target_pairs={{0,8},{8,16},{16,24},{24,32},{32,40},{40,48},{48,56},{56,64},{64,7... | collective-permute-start | bytes 589832 | tf_op jit(solution)/shard_map/while/body/eval_jaxpr/ppermute | solution.py:15
  476.7 76.9 %reduce-scatter.5.cloned.1.call-start = ((), (), s32[]{:S(2)}) async-start(), calls=%async_computation.3 | async-start | bytes 442368 | tf_op jit(solution)/shard_map/reduce_scatter | solution.py:109
  (56 other events, 547.2 us)
Sparse Core Ops, SparseCore 0:
  476.8 52.1 reduce-scatter.2
  531.6 21.9 reduce-scatter.4
where the time goes:
time: 561 us; the launch traced here: 560 us
  waiting for transfers between devices  435 us (78%)
  matrix products  59.9 us (11%)
  starting transfers between devices  24.7 us (4%)
  local copies, waits for them, and re-layouts  21.7 us (4%)
  between operations  13.6 us (2%)
    ppermute x96, waiting for transfers between devices, from_behind(): return lax.ppermute(value, axis, pairs)  358 us
    reduce_scatter x1, waiting for transfers between devices, per_device(): lax.psum_scatter(jnp.einsum('tqc,tdc->qd', grad_qkv, qkv_weight, preferre...  52.3 us
    ppermute x96, starting transfers between devices, from_behind(): return lax.ppermute(value, axis, pairs)  24.7 us
    reduce_scatter x1, waiting for transfers between devices, per_device(): lax.psum_scatter(mine, 'branch', scatter_dimension=1, tiled=True)  24.5 us
    dot_general x16, matrix products, absorb(): jnp.einsum('hqk,khd->hqd', weights, value_block.astype(jnp.float32), prec...  19.8 us
    while x80, local copies, waits for them, and re-layouts  15.6 us
  transfers between devices with their start and end apart: 98, of which 66 were waited for; matrix products, arithmetic and copies ran while one was open for 7% of the time, Pallas kernels for 0%

commit v1 on v0

v1 whole, which is shorter than its diff:
```python
import math

import jax
import jax.numpy as jnp
from jax import lax
from jax.experimental import pallas as pl
from jax.experimental.pallas import tpu as pltpu
from jax.sharding import PartitionSpec as P

HEAD_DIM = 128
GUIDE = 6.0
MESH = pl.DeviceIdType.MESH
BF, F32 = jnp.bfloat16, jnp.float32

ROWS = 384
CHIP = 2 * ROWS
NQ = 4 * CHIP
NK = 2 * CHIP
TILE = 256
TILES = NQ // TILE
CHUNKS = NK // TILE
PER_CHIP = CHIP // TILE
FEAT = 1536
TOK = 48
SCALE = HEAD_DIM**-0.5
TO_EXP2 = SCALE * math.log2(math.e)


def dot(left, right, left_dim, right_dim):
    return lax.dot_general(
        left, right, (((left_dim,), (right_dim,)), ((), ())), preferred_element_type=F32
    )


def eights(value):
    return value.reshape(value.shape[0] // 8, 8, value.shape[1])


def kernel(
    q_in, k_in, v_in, r_in, w_in, out,
    Q, R, K, V, KT, QF, OF, E, DP, DS, SC, W, ST, SG, FD, PQ, PKV,
    XB, XS, YB, YS, BX, BR, GA, PO, ZB, ZS, FS, FR,
    q_sem, r_sem, k_sem, v_sem, g_send, w_sem, st_send, st_recv,
    x_send, x_recv, y_send, y_recv, b_send, b_recv, c_send, c_recv,
    z_send, z_recv, f_send, f_recv,
):
    branch = lax.axis_index("branch")
    blk = lax.axis_index("blk")
    z = lax.axis_index("head")
    core = lax.rem(blk, 2)
    ylo = lax.rem(blk // 2, 2)
    x = blk // 4
    y = 2 * branch + ylo
    other = 1 - core

    def device(dx=0, y_at=None, core_at=None, dz=0):
        y_to = y if y_at is None else y_at
        core_to = core if core_at is None else core_at
        x_to = lax.rem(x + dx + 4, 4)
        return (
            y_to // 2,
            (x_to * 2 + lax.rem(y_to, 2)) * 2 + core_to,
            lax.rem(z + dz + 8, 8),
        )

    y_pair = 2 * branch + (1 - ylo)
    y_far = lax.rem(y + 2, 4)
    y_up = lax.rem(y + 1, 4)
    y_down = lax.rem(y + 3, 4)
    y_rest = 2 * (1 - branch) + (1 - ylo)
    twin = device(core_at=other)

    def copy(src, dst, send, recv, to):
        return pltpu.make_async_remote_copy(
            src_ref=src, dst_ref=dst, send_sem=send, recv_sem=recv, device_id=to, device_id_type=MESH
        )

    def arrived(dst, recv):
        copy(dst, dst, recv, recv, twin).wait_recv()

    partners = [twin, device(dx=2), device(y_at=y_rest), device(y_at=y_far), device(dz=1), device(dz=-1)]
    partners += [device(y_at=y_far, core_at=other)]
    for at in (core, other):
        partners += [device(dx=1, core_at=at), device(dx=-1, core_at=at), device(y_at=y_pair, core_at=at)]
    barrier = pltpu.get_barrier_semaphore()
    for partner in partners:
        pl.semaphore_signal(barrier, inc=1, device_id=partner, device_id_type=MESH)

    mine = pl.ds(pl.multiple_of(core * HEAD_DIM, HEAD_DIM), HEAD_DIM)
    theirs = pl.ds(pl.multiple_of(other * HEAD_DIM, HEAD_DIM), HEAD_DIM)

    def rows_of(slot, half):
        return pl.ds(pl.multiple_of(slot * CHIP + half * ROWS, ROWS), ROWS)

    own = rows_of(0, core)
    local = [
        pltpu.make_async_copy(q_in.at[0, :, mine], Q.at[own], q_sem.at[0, core]),
        pltpu.make_async_copy(r_in.at[:, mine], R.at[own], r_sem.at[0, core]),
        pltpu.make_async_copy(k_in.at[0, :, mine], K.at[own], k_sem.at[0, core]),
        pltpu.make_async_copy(v_in.at[0, :, mine], V.at[own], v_sem.at[0, core]),
    ]
    for each in local:
        each.start()
    w_copy = pltpu.make_async_copy(
        w_in.at[:, pl.ds(pl.multiple_of(core * FEAT, FEAT), FEAT), :], W, w_sem
    )
    w_copy.start()
    ST[...] = jnp.zeros_like(ST)

    pl.semaphore_wait(barrier, len(partners))

    sends = []

    def send(src, dst, recv, to):
        item = copy(src, dst, g_send.at[len(sends)], recv, to)
        item.start()
        sends.append(item)

    q_of, r_of = q_in.at[0], r_in
    turn = 1 - 2 * core
    for step, (dx, slot) in enumerate(((turn, 3 - 2 * core), (-turn, 1 + 2 * core))):
        for cols, at in ((mine, core), (theirs, other)):
            to = device(dx=dx, core_at=at)
            send(q_of.at[:, cols], Q.at[rows_of(slot, core)], q_sem.at[slot, core], to)
            send(r_of.at[:, cols], R.at[rows_of(slot, core)], r_sem.at[slot, core], to)
            if step == 0:
                to = device(y_at=y_pair, core_at=at)
                send(k_in.at[0, :, cols], K.at[rows_of(1, core)], k_sem.at[1, core], to)
                send(v_in.at[0, :, cols], V.at[rows_of(1, core)], v_sem.at[1, core], to)
        if step == 0:
            send(q_of.at[:, theirs], Q.at[own], q_sem.at[0, core], twin)
            send(r_of.at[:, theirs], R.at[own], r_sem.at[0, core], twin)
            send(k_in.at[0, :, theirs], K.at[own], k_sem.at[0, core], twin)
            send(v_in.at[0, :, theirs], V.at[own], v_sem.at[0, core], twin)

    def wait_q(slot, half):
        arrived(Q.at[rows_of(slot, half)], q_sem.at[slot, half])

    def wait_r(slot, half):
        arrived(R.at[rows_of(slot, half)], r_sem.at[slot, half])

    for slot, half, dx in ((3, 0, 1), (1, 1, -1)):
        wait_q(slot, half)
        send(Q.at[rows_of(slot, half)], Q.at[rows_of(2, half)], q_sem.at[2, half], device(dx=dx))
        wait_r(slot, half)
        send(R.at[rows_of(slot, half)], R.at[rows_of(2, half)], r_sem.at[2, half], device(dx=dx))

    for each in local:
        each.wait()
    wait_q(0, other)
    wait_r(0, other)
    arrived(K.at[rows_of(0, other)], k_sem.at[0, other])
    arrived(V.at[rows_of(0, other)], v_sem.at[0, other])
    for half in range(2):
        arrived(K.at[rows_of(1, half)], k_sem.at[1, half])
        arrived(V.at[rows_of(1, half)], v_sem.at[1, half])
    for slot, half in ((3, 1), (1, 0)):
        wait_q(slot, half)
        wait_r(slot, half)
    KT[...] = K[...].T

    coef = jnp.where(branch == 0, 1.0 - GUIDE, GUIDE).astype(F32)

    def chunk(i):
        return pl.ds(i * TILE, TILE)

    def first_pass(turn, _):
        slot = jnp.where(turn < 2, turn, 5 - turn)

        @pl.when(turn == 3)
        def _():
            for half in range(2):
                wait_q(2, half)
                wait_r(2, half)
            for item in sends:
                item.wait_send()

        stat = lax.rem(x + slot, 4) * PER_CHIP

        def scores(t):
            rows = pl.ds(pl.multiple_of(slot * CHIP + t * TILE, TILE), TILE)
            q_tile = Q[rows, :]
            top = None
            for i in range(CHUNKS):
                s = dot(K[chunk(i), :], q_tile, 1, 1)
                SC[t, chunk(i), :] = s
                part = jnp.max(eights(s), axis=0)
                top = part if top is None else jnp.maximum(top, part)
            return jnp.max(top, axis=0, keepdims=True)

        def rest(t, top):
            tile = slot * PER_CHIP + t
            rows = pl.ds(pl.multiple_of(slot * CHIP + t * TILE, TILE), TILE)
            o_tile = (coef * R[rows, :].astype(F32)).astype(BF)
            OF[rows, :] = o_tile
            total, cross = jnp.zeros((8, TILE), F32), jnp.zeros((8, TILE), F32)
            for i in range(CHUNKS):
                e = jnp.exp2((SC[t, chunk(i), :] - top) * TO_EXP2)
                p = dot(V[chunk(i), :], o_tile, 1, 1)
                E[tile, chunk(i), :] = e.astype(BF)
                DP[tile, chunk(i), :] = p
                total += jnp.sum(eights(e), axis=0)
                cross += jnp.sum(eights(e * p), axis=0)
            at = pl.ds(stat + t, 1)
            ST[0, at, :] = top
            ST[1, at, :] = jnp.sum(total, axis=0, keepdims=True)
            ST[2, at, :] = jnp.sum(cross, axis=0, keepdims=True)

        tops = [scores(0)]
        for t in range(PER_CHIP):
            if t + 1 < PER_CHIP:
                tops.append(scores(t + 1))
            rest(t, tops[t])
        return 0

    lax.fori_loop(0, 4, first_pass, 0)

    stat_sends = []
    for i, dx in enumerate((2, 1, 3)):
        item = copy(ST, SG.at[i], st_send.at[i], st_recv.at[i], device(dx=dx))
        item.start()
        stat_sends.append(item)
    for item in stat_sends:
        item.wait()
    top = ST[0]
    for i in range(3):
        top = jnp.maximum(top, SG[i, 0])
    here = jnp.exp2((ST[0] - top) * TO_EXP2)
    total, cross = here * ST[1], here * ST[2]
    for i in range(3):
        fade = jnp.exp2((SG[i, 0] - top) * TO_EXP2)
        total += fade * SG[i, 1]
        cross += fade * SG[i, 2]
    FD[0] = here / total
    FD[1] = cross / total

    def second_pass(turn, _):
        slot = jnp.where(turn == 0, 2, jnp.where(turn == 1, 1, jnp.where(turn == 2, 3, 0)))
        stat = lax.rem(x + slot, 4) * PER_CHIP
        for t in range(PER_CHIP):
            tile = slot * PER_CHIP + t
            rows = pl.ds(pl.multiple_of(slot * CHIP + t * TILE, TILE), TILE)
            at = pl.ds(stat + t, 1)
            f, delta = FD[0, at, :], FD[1, at, :]
            for i in range(CHUNKS):
                ds = E[tile, chunk(i), :].astype(F32) * (DP[tile, chunk(i), :] - delta)
                DS[tile, chunk(i), :] = ds.astype(BF)
            part = dot(KT[...], DS[tile], 1, 0) * (f * SCALE)
            PQ[rows, :] = part.T.astype(BF)
            column = jnp.broadcast_to(f, (HEAD_DIM, TILE)).T
            OF[rows, :] = (OF[rows, :].astype(F32) * column).astype(BF)
            QF[rows, :] = (Q[rows, :].astype(F32) * (column * SCALE)).astype(BF)
        return 0

    lax.fori_loop(0, 4, second_pass, 0)

    class Ring:
        def __init__(self, part, landed, staged, send_sems, recv_sems, to):
            self.part, self.landed, self.staged = part, landed, staged
            self.send_sems, self.recv_sems, self.to = send_sems, recv_sems, to
            self.items = []

        def start(self, way, far, half, src):
            slot = 0 if far else 1 + half
            item = copy(
                src, self.landed.at[way, slot], self.send_sems.at[way, slot],
                self.recv_sems.at[way, slot], self.to[way],
            )
            item.start()
            self.items.append(item)

        def far(self, way):
            self.start(way, True, way, self.part(2, way))

        def plain(self, way):
            self.start(way, False, 1 - way, self.part(1 + 2 * way, 1 - way))

        def relay(self, way):
            arrived(self.landed.at[way, 0], self.recv_sems.at[way, 0])
            mid = self.part(1 + 2 * way, way)[...].astype(F32) + self.landed[way, 0].astype(F32)
            self.staged[way] = mid.astype(BF)
            self.start(way, False, way, self.staged.at[way])

        def total(self, half):
            for way in range(2):
                arrived(self.landed.at[way, 1 + half], self.recv_sems.at[way, 1 + half])
            return (
                self.part(0, half)[...].astype(F32)
                + self.landed[0, 1 + half].astype(F32)
                + self.landed[1, 1 + half].astype(F32)
            )

        def finish(self):
            for item in self.items:
                item.wait_send()

    xr = Ring(
        lambda slot, half: PQ.at[rows_of(slot, half)],
        XB, XS, x_send, x_recv, (device(dx=1), device(dx=-1)),
    )
    for way in range(2):
        xr.far(way)
        xr.plain(way)

    def third_pass(i, _):
        rows = pl.ds(pl.multiple_of(i * TILE, TILE), TILE)
        grad_v, grad_k = jnp.zeros((TILE, HEAD_DIM), F32), jnp.zeros((TILE, HEAD_DIM), F32)
        for t in range(TILES):
            grad_v += dot(E[t, rows, :], OF[chunk(t), :], 1, 0)
            grad_k += dot(DS[t, rows, :], QF[chunk(t), :], 1, 0)
        PKV[0, rows, :] = grad_v.astype(BF)
        PKV[1, rows, :] = grad_k.astype(BF)
        return 0

    lax.fori_loop(0, CHUNKS // 2, third_pass, 0)
    for way in range(2):
        xr.relay(way)
    lax.fori_loop(CHUNKS // 2, CHUNKS, third_pass, 0)

    owners = (branch, y_up // 2, 1 - branch, y_down // 2)
    yr = Ring(
        lambda slot, half: PKV.at[half, rows_of(0 if slot % 2 == 0 else 1, owners[slot])],
        YB, YS, y_send, y_recv, (device(y_at=y_up), device(y_at=y_down)),
    )
    for way in range(2):
        yr.far(way)
        yr.plain(way)

    for half in range(2):
        BX[half] = xr.total(half).astype(BF)
    cross_copy = copy(BX.at[1 - branch], BR, b_send, b_recv, device(y_at=y_far))
    cross_copy.start()
    for way in range(2):
        yr.relay(way)
    cross_copy.wait_recv()
    GA[core, 0] = (BX[branch].astype(F32) + BR[...].astype(F32)).astype(BF)
    GA[core, 2] = yr.total(0).astype(BF)
    GA[core, 1] = yr.total(1).astype(BF)
    swap = copy(GA.at[core], GA.at[core], c_send, c_recv, twin)
    swap.start()
    arrived(GA.at[other], c_recv)
    w_copy.wait()

    def project(i, _):
        feats = pl.ds(pl.multiple_of(i * TILE, TILE), TILE)
        total = jnp.zeros((ROWS, TILE), F32)
        for which in range(3):
            both = jnp.concatenate([GA[0, which], GA[1, which]], axis=1)
            total += dot(both, W[which, feats, :], 1, 1)
        PO[:, feats] = total.astype(BF)
        return 0

    lax.fori_loop(0, FEAT // TILE, project, 0)

    z_to = (device(dz=1), device(dz=-1))
    z_items = []
    width = FEAT // 2

    def z_part(way, dist, half):
        at = lax.rem(z + (dist if way == 0 else 8 - dist), 8)
        return PO.at[pl.ds(pl.multiple_of(at * TOK, 16), TOK), pl.ds(half * width, width)]

    def z_start(way, dist, half, src):
        item = copy(
            src, ZB.at[way, dist - 1, half], z_send.at[way, dist - 1, half],
            z_recv.at[way, dist - 1, half], z_to[way],
        )
        item.start()
        z_items.append(item)

    for way in range(2):
        z_start(way, 4, way, z_part(way, 4, way))
    for way in range(2):
        z_start(way, 3, 1 - way, z_part(way, 3, 1 - way))
    for dist in (3, 2, 1):
        for first in range(2):
            for way in range(2):
                half = way if first == 0 else 1 - way
                if dist == 3 and half != way:
                    continue
                arrived(ZB.at[way, dist, half], z_recv.at[way, dist, half])
                mid = z_part(way, dist, half)[...].astype(F32) + ZB[way, dist, half].astype(F32)
                ZS[way, dist - 1, half] = mid.astype(BF)
                z_start(way, dist, half, ZS.at[way, dist - 1, half])
    for half in range(2):
        for way in range(2):
            arrived(ZB.at[way, 0, half], z_recv.at[way, 0, half])
        done = (
            z_part(0, 0, half)[...].astype(F32)
            + ZB[0, 0, half].astype(F32)
            + ZB[1, 0, half].astype(F32)
        )
        FS[:, pl.ds(half * width, width)] = done.astype(BF)

    @pl.when(branch == core)
    def _():
        out[...] = FS[...]

    @pl.when(branch != core)
    def _():
        last = copy(FS, FR, f_send, f_recv, device(y_at=y_far, core_at=other))
        last.start()
        last.wait()
        out[...] = FR[...]

    xr.finish()
    yr.finish()
    cross_copy.wait_send()
    swap.wait_send()
    for item in z_items:
        item.wait_send()


def per_device(queries, keys, values, reward_grad, qkv_weight):
    def vm(*shape, dtype=BF):
        return pltpu.VMEM(shape, dtype)

    dma = pltpu.SemaphoreType.DMA
    scratch = [
        vm(NQ, HEAD_DIM), vm(NQ, HEAD_DIM), vm(NK, HEAD_DIM), vm(NK, HEAD_DIM),
        vm(HEAD_DIM, NK), vm(NQ, HEAD_DIM), vm(NQ, HEAD_DIM),
        vm(TILES, NK, TILE), vm(TILES, NK, TILE, dtype=F32), vm(TILES, NK, TILE),
        vm(PER_CHIP, NK, TILE, dtype=F32), vm(3, FEAT, 2 * HEAD_DIM),
        vm(3, 16, TILE, dtype=F32), vm(3, 3, 16, TILE, dtype=F32), vm(2, 16, TILE, dtype=F32),
        vm(NQ, HEAD_DIM), vm(2, NK, HEAD_DIM),
        vm(2, 3, ROWS, HEAD_DIM), vm(2, ROWS, HEAD_DIM),
        vm(2, 3, ROWS, HEAD_DIM), vm(2, ROWS, HEAD_DIM),
        vm(2, ROWS, HEAD_DIM), vm(ROWS, HEAD_DIM), vm(2, 3, ROWS, HEAD_DIM),
        vm(ROWS, FEAT), vm(2, 4, 2, TOK, FEAT // 2), vm(2, 3, 2, TOK, FEAT // 2),
        vm(TOK, FEAT), vm(TOK, FEAT),
        dma((4, 2)), dma((4, 2)), dma((2, 2)), dma((2, 2)), dma((20,)), dma(()),
        dma((3,)), dma((3,)), dma((2, 3)), dma((2, 3)), dma((2, 3)), dma((2, 3)),
        dma(()), dma(()), dma(()), dma(()), dma((2, 4, 2)), dma((2, 4, 2)), dma(()), dma(()),
    ]
    return pl.pallas_call(
        kernel,
        out_shape=jax.ShapeDtypeStruct((TOK, FEAT), BF),
        in_specs=[pl.BlockSpec(memory_space=pl.ANY)] * 5,
        out_specs=pl.BlockSpec(memory_space=pltpu.VMEM),
        scratch_shapes=scratch,
        compiler_params=pltpu.CompilerParams(
            collective_id=0, has_side_effects=True, vmem_limit_bytes=62 * 2**20
        ),
    )(queries, keys, values, reward_grad, qkv_weight)


def solution(mesh):
    placed = (
        P("branch", "blk", "head"),
        P("branch", "blk", "head"),
        P("branch", "blk", "head"),
        P("blk", "head"),
        P(None, None, "head"),
    )
    return jax.shard_map(
        per_device,
        mesh=mesh,
        in_specs=placed,
        out_specs=P(("blk", "head"), "branch"),
        check_vma=False,
    )
```

time: 561 us -> 81.9 us (0.15)
  waiting for transfers between devices: 435 us -> 0 us
  Pallas kernels: 0 us -> 80.2 us
  matrix products: 59.9 us -> 0 us
  starting transfers between devices: 24.7 us -> 0 us
  local copies, waits for them, and re-layouts: 21.7 us -> 1.58 us
  between operations: 13.6 us -> 0.01 us
    ppermute x96 -> x0, waiting for transfers between devices: 358 us -> none  [from_behind(): return lax.ppermute(value, axis, pairs)]
    pallas_call x0 -> x1, Pallas kernels: none -> 80.2 us  [per_device(): pl.pallas_call(kernel, out_shape=jax.ShapeDtypeStruct((TOK, FEAT), BF), i...]
    reduce_scatter x2 -> x0, waiting for transfers between devices: 76.8 us -> none  [the longest x1 52.3 us: per_device(): lax.psum_scatter(jnp.einsum('tqc,tdc->qd', grad_qkv, qkv_weight, preferre...]
    dot_general x113 -> x0, matrix products: 59.9 us -> none  [the longest x16 19.8 us: absorb(): jnp.einsum('hqk,khd->hqd', weights, value_block.astype(jnp.float32), prec...]
    ppermute x96 -> x0, starting transfers between devices: 24.7 us -> none  [from_behind(): return lax.ppermute(value, axis, pairs)]
    while x80 -> x0, local copies, waits for them, and re-layouts: 15.6 us -> none
  transfers between devices with their start and end apart: 98 -> 0, of which waited for: 66 -> 0; matrix products, arithmetic and copies ran while one was open for 7% -> 0% of each run, Pallas kernels for 0% -> 0%
where the time goes in v1:
time: 81.9 us; the launch traced here: 81.8 us
  Pallas kernels  80.2 us (98%)
  local copies, waits for them, and re-layouts  1.58 us (2%)
    pallas_call x1, Pallas kernels, per_device(): pl.pallas_call(kernel, out_shape=jax.ShapeDtypeStruct((TOK, FEAT), BF), i...  80.2 us

profile of v1, /device:TPU:1, one launch (start us, length us, event | category | flops | bytes accessed | tf_op | source)
XLA Modules:
  0.0 81.8 jit_solution(11542702578731419514)
XLA Ops:
  0.0 80.2 %shard_map.55 = bf16[48,1536]{1,0:T(8,128)(2,1)} custom-call(bf16[1,384,256]{2,1,0:T(8,128)(2,1)} %q_in.1, bf16[1,384,256]{2,1,0:T(8,128)(2,1)} %k_in.1, bf16[1,384,256]{2,1,0:T(8,128)(2,1)} %v_in.1, bf16[384,256]{1,0:T(8,128)(2,1)} %r_in.1, bf16[3,3072,256]{2,1,0:T(8,128)(2,1)} %w_in.1), custom_call_target="tpu_custom_call" | custom-call | tf_op jit(solution)/shard_map/pallas_call | solution.py:435
  80.2 1.6 %copy.7 = bf16[48,1536]{1,0:T(8,128)(2,1)} copy(bf16[48,1536]{1,0:T(8,128)(2,1)} %shard_map.55) | data formatting | bytes 294912

commit v2 on v1

v2 whole, which is shorter than its diff:
```python
import math

import jax
import jax.numpy as jnp
from jax import lax
from jax.experimental import pallas as pl
from jax.experimental.pallas import tpu as pltpu
from jax.sharding import PartitionSpec as P

HEAD_DIM = 128
GUIDE = 6.0
MESH = pl.DeviceIdType.MESH
BF, F32 = jnp.bfloat16, jnp.float32

ROWS = 384
CHIP = 2 * ROWS
NQ = 4 * CHIP
NK = 2 * CHIP
TILE = 256
WIDE = 1024
TILES = NQ // TILE
CHUNKS = NK // TILE
PER_CHIP = CHIP // TILE
FEAT = 1536
TOK = 48
SUBS = 1
SCALE = HEAD_DIM**-0.5
TO_EXP2 = SCALE * math.log2(math.e)


def dot(left, right, left_dim, right_dim):
    return lax.dot_general(
        left, right, (((left_dim,), (right_dim,)), ((), ())), preferred_element_type=F32
    )


def eights(value):
    return value.reshape(value.shape[0] // 8, 8, value.shape[1])


def kernel(
    q_in, k_in, v_in, r_in, w_in, out,
    Q, R, K, V, KT, QF, OG, E, DS, SC, DP, X, Y, W, ST, SG, FD, PQ, PKV,
    XB, YB, BX, BR, GA, PF, PO, ZB, ZS, ZF, ZO,
    q_sem, r_sem, k_sem, v_sem, g_send, w_sem, st_send, st_recv,
    x_send, x_recv, y_send, y_recv, b_send, b_recv, c_send, c_recv,
    z_send, z_recv, f_send, f_recv,
):
    branch = lax.axis_index("branch")
    blk = lax.axis_index("blk")
    z = lax.axis_index("head")
    core = lax.rem(blk, 2)
    ylo = lax.rem(blk // 2, 2)
    x = blk // 4
    y = 2 * branch + ylo
    other = 1 - core

    def device(dx=0, y_at=None, core_at=None, dz=0):
        y_to = y if y_at is None else y_at
        core_to = core if core_at is None else core_at
        x_to = lax.rem(x + dx + 4, 4)
        return (
            y_to // 2,
            (x_to * 2 + lax.rem(y_to, 2)) * 2 + core_to,
            lax.rem(z + dz + 8, 8),
        )

    y_pair = 2 * branch + (1 - ylo)
    y_far = lax.rem(y + 2, 4)
    y_up = lax.rem(y + 1, 4)
    y_down = lax.rem(y + 3, 4)
    y_rest = 2 * (1 - branch) + (1 - ylo)
    twin = device(core_at=other)

    def copy(src, dst, send, recv, to):
        return pltpu.make_async_remote_copy(
            src_ref=src, dst_ref=dst, send_sem=send, recv_sem=recv, device_id=to, device_id_type=MESH
        )

    def arrived(dst, recv):
        copy(dst, dst, recv, recv, twin).wait_recv()

    partners = [twin, device(y_at=y_rest), device(y_at=y_far), device(dz=1), device(dz=-1)]
    for at in (core, other):
        partners += [device(dx=1, core_at=at), device(dx=-1, core_at=at), device(y_at=y_pair, core_at=at)]
    barrier = pltpu.get_barrier_semaphore()
    for partner in partners:
        pl.semaphore_signal(barrier, inc=1, device_id=partner, device_id_type=MESH)

    mine = pl.ds(pl.multiple_of(core * HEAD_DIM, HEAD_DIM), HEAD_DIM)
    theirs = pl.ds(pl.multiple_of(other * HEAD_DIM, HEAD_DIM), HEAD_DIM)

    def rows_of(slot, half):
        return pl.ds(pl.multiple_of(slot * CHIP + half * ROWS, ROWS), ROWS)

    own = rows_of(0, core)
    local = [
        pltpu.make_async_copy(q_in.at[0, :, mine], Q.at[own], q_sem.at[0, core]),
        pltpu.make_async_copy(r_in.at[:, mine], R.at[own], r_sem.at[0, core]),
        pltpu.make_async_copy(k_in.at[0, :, mine], K.at[own], k_sem.at[0, core]),
        pltpu.make_async_copy(v_in.at[0, :, mine], V.at[own], v_sem.at[0, core]),
    ]
    for each in local:
        each.start()
    w_copy = pltpu.make_async_copy(
        w_in.at[:, pl.ds(pl.multiple_of(core * FEAT, FEAT), FEAT), :], W, w_sem
    )
    w_copy.start()
    ST[...] = jnp.zeros_like(ST)

    pl.semaphore_wait(barrier, len(partners))

    sends = []

    def send(src, dst, recv, to):
        item = copy(src, dst, g_send.at[len(sends)], recv, to)
        item.start()
        sends.append(item)

    q_of, r_of = q_in.at[0], r_in
    turn = 1 - 2 * core
    for step, (dx, slot) in enumerate(((turn, 3 - 2 * core), (-turn, 1 + 2 * core))):
        there = rows_of(slot, core)
        for cols, at in ((theirs, other), (mine, core)):
            send(q_of.at[:, cols], Q.at[there], q_sem.at[slot, core], device(dx=dx, core_at=at))
        for cols, at in ((theirs, other), (mine, core)):
            send(r_of.at[:, cols], R.at[there], r_sem.at[slot, core], device(dx=dx, core_at=at))
        if step == 0:
            there = rows_of(1, core)
            for cols, at in ((theirs, other), (mine, core)):
                to = device(y_at=y_pair, core_at=at)
                send(k_in.at[0, :, cols], K.at[there], k_sem.at[1, core], to)
                send(v_in.at[0, :, cols], V.at[there], v_sem.at[1, core], to)
            send(q_of.at[:, theirs], Q.at[own], q_sem.at[0, core], twin)
            send(r_of.at[:, theirs], R.at[own], r_sem.at[0, core], twin)
            send(k_in.at[0, :, theirs], K.at[own], k_sem.at[0, core], twin)
            send(v_in.at[0, :, theirs], V.at[own], v_sem.at[0, core], twin)

    def wait_q(slot, half):
        arrived(Q.at[rows_of(slot, half)], q_sem.at[slot, half])

    def wait_r(slot, half):
        arrived(R.at[rows_of(slot, half)], r_sem.at[slot, half])

    relays = ((3, 0, 1), (1, 1, -1))
    for slot, half, dx in relays:
        wait_q(slot, half)
        send(Q.at[rows_of(slot, half)], Q.at[rows_of(2, half)], q_sem.at[2, half], device(dx=dx))
    for slot, half, dx in relays:
        wait_r(slot, half)
        send(R.at[rows_of(slot, half)], R.at[rows_of(2, half)], r_sem.at[2, half], device(dx=dx))

    for each in local:
        each.wait()
    wait_q(0, other)
    wait_r(0, other)
    arrived(K.at[rows_of(0, other)], k_sem.at[0, other])
    arrived(V.at[rows_of(0, other)], v_sem.at[0, other])
    for half in range(2):
        arrived(K.at[rows_of(1, half)], k_sem.at[1, half])
        arrived(V.at[rows_of(1, half)], v_sem.at[1, half])
    for slot, half in ((3, 1), (1, 0)):
        wait_q(slot, half)
        wait_r(slot, half)
    KT[...] = K[...].T

    coef = jnp.where(branch == 0, 1.0 - GUIDE, GUIDE).astype(F32)

    def chunk(i):
        return pl.ds(i * TILE, TILE)

    def tile_at(slot, t):
        return pl.ds(pl.multiple_of(slot * CHIP + t * TILE, TILE), TILE)

    stat_offsets = (2, 1, 3)

    def stat_copies(chip):
        return [
            copy(ST.at[chip], SG.at[i, chip], st_send.at[i, chip], st_recv.at[i, chip], device(dx=dx))
            for i, dx in enumerate(stat_offsets)
        ]

    def first_pass(turn, _):
        slot = jnp.where(turn < 2, turn, 5 - turn)
        chip = lax.rem(x + slot, 4)

        @pl.when(turn == 3)
        def _():
            for half in range(2):
                wait_q(2, half)
                wait_r(2, half)

        def scores(t):
            q_tile = Q[tile_at(slot, t), :]
            top = None
            for i in range(CHUNKS):
                s = dot(K[chunk(i), :], q_tile, 1, 1)
                SC[t, chunk(i), :] = s
                part = jnp.max(eights(s), axis=0)
                top = part if top is None else jnp.maximum(top, part)
            return jnp.max(top, axis=0, keepdims=True)

        def sums(t, top):
            cols = tile_at(slot, t)
            o_tile = (coef * R[cols, :].astype(F32)).astype(BF)
            OG[cols, :HEAD_DIM] = o_tile
            total, cross = jnp.zeros((8, TILE), F32), jnp.zeros((8, TILE), F32)
            for i in range(CHUNKS):
                e = jnp.exp2((SC[t, chunk(i), :] - top) * TO_EXP2)
                p = dot(V[chunk(i), :], o_tile, 1, 1)
                E[chunk(i), cols] = e.astype(BF)
                SC[t, chunk(i), :] = e
                DP[t, chunk(i), :] = p
                total += jnp.sum(eights(e), axis=0)
                cross += jnp.sum(eights(e * p), axis=0)
            total = jnp.sum(total, axis=0, keepdims=True)
            cross = jnp.sum(cross, axis=0, keepdims=True)
            ST[chip, 0:1, chunk(t)] = top
            ST[chip, 1:2, chunk(t)] = total
            ST[chip, 2:3, chunk(t)] = cross
            return cross / total

        def grads(t, delta):
            cols = tile_at(slot, t)
            for i in range(CHUNKS):
                ds = SC[t, chunk(i), :] * (DP[t, chunk(i), :] - delta)
                DS[chunk(i), cols] = ds.astype(BF)

        tops = [scores(0), scores(1)]
        deltas = [sums(0, tops[0])]
        tops.append(scores(2))
        deltas.append(sums(1, tops[1]))
        grads(0, deltas[0])
        deltas.append(sums(2, tops[2]))
        for item in stat_copies(chip):
            item.start()
        grads(1, deltas[1])
        grads(2, deltas[2])
        return 0

    lax.fori_loop(0, 4, first_pass, 0)

    def key_products(i, _):
        cols = pl.ds(pl.multiple_of(i * WIDE, WIDE), WIDE)
        X[:, cols] = dot(KT[...], DS[:, cols], 1, 0)
        Y[:, cols] = dot(KT[...], E[:, cols], 1, 0)
        return 0

    lax.fori_loop(0, NQ // WIDE, key_products, 0)

    for chip in range(4):
        for item in stat_copies(chip):
            item.wait()
        top, total, cross = (ST[chip, k : k + 1, :] for k in range(3))
        whole = top
        for i in range(3):
            whole = jnp.maximum(whole, SG[i, chip, 0:1, :])
        here = jnp.exp2((top - whole) * TO_EXP2)
        total_all, cross_all = here * total, here * cross
        for i in range(3):
            fade = jnp.exp2((SG[i, chip, 0:1, :] - whole) * TO_EXP2)
            total_all += fade * SG[i, chip, 1:2, :]
            cross_all += fade * SG[i, chip, 2:3, :]
        FD[chip, 0:1, :] = here / total_all
        FD[chip, 1:2, :] = cross / total - cross_all / total_all

    def second_pass(turn, _):
        slot = jnp.where(turn == 0, 2, jnp.where(turn == 1, 1, jnp.where(turn == 2, 3, 0)))
        chip = lax.rem(x + slot, 4)
        for t in range(PER_CHIP):
            cols = tile_at(slot, t)
            f, shift = FD[chip, 0:1, chunk(t)], FD[chip, 1:2, chunk(t)]
            part = (X[:, cols] + shift * Y[:, cols]) * (f * SCALE)
            PQ[cols, :] = part.T.astype(BF)
            f_col = jnp.broadcast_to(f, (HEAD_DIM, TILE)).T
            s_col = jnp.broadcast_to(shift, (HEAD_DIM, TILE)).T
            q_tile = Q[cols, :].astype(F32) * (f_col * SCALE)
            QF[cols, :] = q_tile.astype(BF)
            OG[cols, HEAD_DIM:] = (q_tile * s_col).astype(BF)
            OG[cols, :HEAD_DIM] = (OG[cols, :HEAD_DIM].astype(F32) * f_col).astype(BF)
        return 0

    lax.fori_loop(0, 4, second_pass, 0)

    x_items = []
    for step, half in enumerate((1 - branch, branch)):
        for i, dx in enumerate((2, 1, 3)):
            item = copy(
                PQ.at[rows_of(dx, half)], XB.at[step, i], x_send.at[step, i], x_recv.at[step, i], device(dx=dx)
            )
            item.start()
            x_items.append(item)

    def y_copy(i):
        to = device(y_at=lax.rem(y + jnp.where(i == 0, 2, jnp.where(i == 1, 1, 3)), 4))
        return copy(PKV.at[i], YB.at[i], y_send.at[i], y_recv.at[i], to)

    def third_pass(i, _):
        slot = jnp.where((i == 1) | (i == 2), 1, 0)
        half = jnp.where(
            i == 0, 1 - branch, jnp.where(i == 1, y_up // 2, jnp.where(i == 2, y_down // 2, branch))
        )
        rows = rows_of(slot, half)
        both = dot(E[rows, :], OG[...], 1, 0)
        grad_k = dot(DS[rows, :], QF[...], 1, 0) + both[:, HEAD_DIM:]
        PKV[i, 0] = grad_k.astype(BF)
        PKV[i, 1] = both[:, :HEAD_DIM].astype(BF)

        @pl.when(i < 3)
        def _():
            y_copy(i).start()

        return 0

    lax.fori_loop(0, 4, third_pass, 0)

    def x_sum(step, half):
        total = PQ[rows_of(0, half), :].astype(F32)
        for i in range(3):
            arrived(XB.at[step, i], x_recv.at[step, i])
            total += XB[step, i].astype(F32)
        return total

    BX[...] = x_sum(0, 1 - branch).astype(BF)
    cross_copy = copy(BX, BR, b_send, b_recv, device(y_at=y_far))
    cross_copy.start()
    total_q = x_sum(1, branch)
    for i in range(3):
        arrived(YB.at[i], y_recv.at[i])
    for k in range(2):
        total = PKV[3, k].astype(F32)
        for i in range(3):
            total += YB[i, k].astype(F32)
        GA[core, 1 + k] = total.astype(BF)
    swap = copy(GA.at[core, pl.ds(1, 2)], GA.at[core, pl.ds(1, 2)], c_send.at[0], c_recv.at[0], twin)
    swap.start()
    cross_copy.wait_recv()
    GA[core, 0] = (total_q + BR[...].astype(F32)).astype(BF)
    swap_q = copy(GA.at[core, 0], GA.at[core, 0], c_send.at[1], c_recv.at[1], twin)
    swap_q.start()
    w_copy.wait()
    arrived(GA.at[other, pl.ds(1, 2)], c_recv.at[0])

    def both_heads(which):
        return jnp.concatenate([GA[0, which], GA[1, which]], axis=1)

    for i in range(FEAT // TILE):
        PF[:, chunk(i)] = dot(both_heads(1), W[1, chunk(i), :], 1, 1) + dot(both_heads(2), W[2, chunk(i), :], 1, 1)
    arrived(GA.at[other, 0], c_recv.at[1])
    for i in range(FEAT // TILE):
        PO[:, chunk(i)] = (PF[:, chunk(i)] + dot(both_heads(0), W[0, chunk(i), :], 1, 1)).astype(BF)

    owner_y, owner_core = 2 * core + ylo, branch
    z_to = (device(dz=1), device(dz=-1))
    end_to = tuple(device(y_at=owner_y, core_at=owner_core, dz=dz) for dz in (1, -1))
    z_items = []
    width = FEAT // 2 // SUBS

    def z_part(way, dist, half, sub):
        at = lax.rem(z + (dist if way == 0 else 8 - dist), 8)
        return PO.at[
            pl.ds(pl.multiple_of(at * TOK, 16), TOK), pl.ds((half * SUBS + sub) * width, width)
        ]

    def z_start(way, dist, half, sub, src):
        place = (way, dist - 1, half, sub)
        item = copy(
            src, ZB.at[place] if dist > 1 else ZF.at[way, half, sub], z_send.at[place], z_recv.at[place],
            z_to[way] if dist > 1 else end_to[way],
        )
        item.start()
        z_items.append(item)

    for sub in range(SUBS):
        for way in range(2):
            z_start(way, 4, way, sub, z_part(way, 4, way, sub))
    for sub in range(SUBS):
        for way in range(2):
            z_start(way, 3, 1 - way, sub, z_part(way, 3, 1 - way, sub))
    at_home = pl.ds(pl.multiple_of(z * TOK, 16), TOK)
    own_part = copy(
        PO.at[at_home], ZO, f_send, f_recv, device(y_at=y_far, core_at=other)
    )

    @pl.when(branch != core)
    def _():
        own_part.start()

    for dist, chain in ((3, 0), (2, 1), (2, 0), (1, 1), (1, 0)):
        for sub in range(SUBS):
            for way in range(2):
                half = way if chain == 0 else 1 - way
                place = (way, dist, half, sub)
                arrived(ZB.at[place], z_recv.at[place])
                mid = z_part(way, dist, half, sub)[...].astype(F32) + ZB[place].astype(F32)
                place = (way, dist - 1, half, sub)
                ZS[place] = mid.astype(BF)
                z_start(way, dist, half, sub, ZS.at[place])

    @pl.when(branch == core)
    def _():
        ZO[...] = PO[at_home, :]

    @pl.when(branch != core)
    def _():
        own_part.wait()

    for half in range(2):
        for sub in range(SUBS):
            cols = pl.ds((half * SUBS + sub) * width, width)
            done = ZO[:, cols].astype(F32)
            for way in range(2):
                arrived(ZF.at[way, half, sub], z_recv.at[way, 0, half, sub])
                done += ZF[way, half, sub].astype(F32)
            out[:, cols] = done.astype(BF)

    for item in sends:
        item.wait_send()
    for item in x_items:
        item.wait_send()
    for i in range(3):
        y_copy(i).wait_send()
    cross_copy.wait_send()
    swap.wait_send()
    swap_q.wait_send()
    for item in z_items:
        item.wait_send()


def per_device(queries, keys, values, reward_grad, qkv_weight):
    def vm(*shape, dtype=BF):
        return pltpu.VMEM(shape, dtype)

    dma = pltpu.SemaphoreType.DMA
    sub = FEAT // 2 // SUBS
    scratch = [
        vm(NQ, HEAD_DIM), vm(NQ, HEAD_DIM), vm(NK, HEAD_DIM), vm(NK, HEAD_DIM),
        vm(HEAD_DIM, NK), vm(NQ, HEAD_DIM), vm(NQ, 2 * HEAD_DIM),
        vm(NK, NQ), vm(NK, NQ),
        vm(PER_CHIP, NK, TILE, dtype=F32), vm(PER_CHIP, NK, TILE, dtype=F32),
        vm(HEAD_DIM, NQ, dtype=F32), vm(HEAD_DIM, NQ, dtype=F32),
        vm(3, FEAT, 2 * HEAD_DIM),
        vm(4, 8, CHIP, dtype=F32), vm(3, 4, 8, CHIP, dtype=F32), vm(4, 8, CHIP, dtype=F32),
        vm(NQ, HEAD_DIM), vm(4, 2, ROWS, HEAD_DIM),
        vm(2, 3, ROWS, HEAD_DIM), vm(3, 2, ROWS, HEAD_DIM),
        vm(ROWS, HEAD_DIM), vm(ROWS, HEAD_DIM), vm(2, 3, ROWS, HEAD_DIM),
        vm(ROWS, FEAT, dtype=F32), vm(ROWS, FEAT),
        vm(2, 4, 2, SUBS, TOK, sub), vm(2, 3, 2, SUBS, TOK, sub),
        vm(2, 2, SUBS, TOK, sub), vm(TOK, FEAT),
        dma((4, 2)), dma((4, 2)), dma((2, 2)), dma((2, 2)), dma((20,)), dma(()),
        dma((3, 4)), dma((3, 4)), dma((2, 3)), dma((2, 3)), dma((3,)), dma((3,)),
        dma(()), dma(()), dma((2,)), dma((2,)), dma((2, 4, 2, SUBS)), dma((2, 4, 2, SUBS)), dma(()), dma(()),
    ]
    return pl.pallas_call(
        kernel,
        out_shape=jax.ShapeDtypeStruct((TOK, FEAT), BF),
        in_specs=[pl.BlockSpec(memory_space=pl.ANY)] * 5,
        out_specs=pl.BlockSpec(memory_space=pltpu.VMEM),
        scratch_shapes=scratch,
        compiler_params=pltpu.CompilerParams(
            collective_id=0, has_side_effects=True, vmem_limit_bytes=62 * 2**20
        ),
    )(queries, keys, values, reward_grad, qkv_weight)


def solution(mesh):
    placed = (
        P("branch", "blk", "head"),
        P("branch", "blk", "head"),
        P("branch", "blk", "head"),
        P("blk", "head"),
        P(None, None, "head"),
    )
    return jax.shard_map(
        per_device,
        mesh=mesh,
        in_specs=placed,
        out_specs=P(("blk", "head"), "branch"),
        check_vma=False,
    )
```

time: 81.9 us -> 73.8 us (0.901)
  Pallas kernels: 80.2 us -> 72.1 us
    pallas_call x1, Pallas kernels: 80.2 us -> 72.1 us  [per_device(): pl.pallas_call(kernel, out_shape=jax.ShapeDtypeStruct((TOK, FEAT), BF), i...]
where the time goes in v2:
time: 73.8 us; the launch traced here: 73.7 us
  Pallas kernels  72.1 us (98%)
  local copies, waits for them, and re-layouts  1.58 us (2%)
    pallas_call x1, Pallas kernels, per_device(): pl.pallas_call(kernel, out_shape=jax.ShapeDtypeStruct((TOK, FEAT), BF), i...  72.1 us
    unnamed x1, local copies, waits for them, and re-layouts  1.58 us

profile of v2, /device:TPU:1, one launch (start us, length us, event | category | flops | bytes accessed | tf_op | source)
XLA Modules:
  0.0 73.7 jit_solution(2136077929951495471)
XLA Ops:
  0.0 72.1 %shard_map.55 = bf16[48,1536]{1,0:T(8,128)(2,1)} custom-call(bf16[1,384,256]{2,1,0:T(8,128)(2,1)} %q_in.1, bf16[1,384,256]{2,1,0:T(8,128)(2,1)} %k_in.1, bf16[1,384,256]{2,1,0:T(8,128)(2,1)} %v_in.1, bf16[384,256]{1,0:T(8,128)(2,1)} %r_in.1, bf16[3,3072,256]{2,1,0:T(8,128)(2,1)} %w_in.1), custom_call_target="tpu_custom_call" | custom-call | tf_op jit(solution)/shard_map/pallas_call | solution.py:454
  72.1 1.6 %copy.7 = bf16[48,1536]{1,0:T(8,128)(2,1)} copy(bf16[48,1536]{1,0:T(8,128)(2,1)} %shard_map.55) | data formatting | bytes 294912

commit v3 on v2

--- a/solution.py
+++ b/solution.py
@@ -17,7 +17,6 @@
 NQ = 4 * CHIP
 NK = 2 * CHIP
 TILE = 256
-WIDE = 1024
 TILES = NQ // TILE
 CHUNKS = NK // TILE
 PER_CHIP = CHIP // TILE
@@ -40,7 +39,7 @@
 
 def kernel(
     q_in, k_in, v_in, r_in, w_in, out,
-    Q, R, K, V, KT, QF, OG, E, DS, SC, DP, X, Y, W, ST, SG, FD, PQ, PKV,
+    Q, R, K, V, KT, QF, OF, E, DS, SC, DP, W, ST, SG, FD, PQ, PKV,
     XB, YB, BX, BR, GA, PF, PO, ZB, ZS, ZF, ZO,
     q_sem, r_sem, k_sem, v_sem, g_send, w_sem, st_send, st_recv,
     x_send, x_recv, y_send, y_recv, b_send, b_recv, c_send, c_recv,
@@ -117,24 +116,26 @@
         item.start()
         sends.append(item)
 
-    q_of, r_of = q_in.at[0], r_in
-    turn = 1 - 2 * core
-    for step, (dx, slot) in enumerate(((turn, 3 - 2 * core), (-turn, 1 + 2 * core))):
-        there = rows_of(slot, core)
-        for cols, at in ((theirs, other), (mine, core)):
-            send(q_of.at[:, cols], Q.at[there], q_sem.at[slot, core], device(dx=dx, core_at=at))
-        for cols, at in ((theirs, other), (mine, core)):
-            send(r_of.at[:, cols], R.at[there], r_sem.at[slot, core], device(dx=dx, core_at=at))
-        if step == 0:
-            there = rows_of(1, core)
-            for cols, at in ((theirs, other), (mine, core)):
-                to = device(y_at=y_pair, core_at=at)
-                send(k_in.at[0, :, cols], K.at[there], k_sem.at[1, core], to)
-                send(v_in.at[0, :, cols], V.at[there], v_sem.at[1, core], to)
-            send(q_of.at[:, theirs], Q.at[own], q_sem.at[0, core], twin)
-            send(r_of.at[:, theirs], R.at[own], r_sem.at[0, core], twin)
-            send(k_in.at[0, :, theirs], K.at[own], k_sem.at[0, core], twin)
-            send(v_in.at[0, :, theirs], V.at[own], v_sem.at[0, core], twin)
+    heads = ((theirs, other), (mine, core))
+    pair = rows_of(1, core)
+    for first in range(2):
+        for cols, at in heads:
+            for dx, slot, queries in ((1, 3, first == 0), (-1, 1, first == 1)):
+                there, to = rows_of(slot, core), device(dx=dx, core_at=at)
+                if queries:
+                    send(q_in.at[0, :, cols], Q.at[there], q_sem.at[slot, core], to)
+                else:
+                    send(r_in.at[:, cols], R.at[there], r_sem.at[slot, core], to)
+            to = device(y_at=y_pair, core_at=at)
+            if first == 0:
+                send(k_in.at[0, :, cols], K.at[pair], k_sem.at[1, core], to)
+            else:
+                send(v_in.at[0, :, cols], V.at[pair], v_sem.at[1, core], to)
+
+    send(k_in.at[0, :, theirs], K.at[own], k_sem.at[0, core], twin)
+    send(v_in.at[0, :, theirs], V.at[own], v_sem.at[0, core], twin)
+    send(q_in.at[0, :, theirs], Q.at[own], q_sem.at[0, core], twin)
+    send(r_in.at[:, theirs], R.at[own], r_sem.at[0, core], twin)
 
     def wait_q(slot, half):
         arrived(Q.at[rows_of(slot, half)], q_sem.at[slot, half])
@@ -142,13 +143,11 @@
     def wait_r(slot, half):
         arrived(R.at[rows_of(slot, half)], r_sem.at[slot, half])
 
-    relays = ((3, 0, 1), (1, 1, -1))
-    for slot, half, dx in relays:
-        wait_q(slot, half)
-        send(Q.at[rows_of(slot, half)], Q.at[rows_of(2, half)], q_sem.at[2, half], device(dx=dx))
-    for slot, half, dx in relays:
-        wait_r(slot, half)
-        send(R.at[rows_of(slot, half)], R.at[rows_of(2, half)], r_sem.at[2, half], device(dx=dx))
+    for half in range(2):
+        wait_q(3, half)
+        send(Q.at[rows_of(3, half)], Q.at[rows_of(2, half)], q_sem.at[2, half], device(dx=1))
+        wait_r(1, half)
+        send(R.at[rows_of(1, half)], R.at[rows_of(2, half)], r_sem.at[2, half], device(dx=-1))
 
     for each in local:
         each.wait()
@@ -158,11 +157,6 @@
     arrived(V.at[rows_of(0, other)], v_sem.at[0, other])
     for half in range(2):
         arrived(K.at[rows_of(1, half)], k_sem.at[1, half])
-        arrived(V.at[rows_of(1, half)], v_sem.at[1, half])
-    for slot, half in ((3, 1), (1, 0)):
-        wait_q(slot, half)
-        wait_r(slot, half)
-    KT[...] = K[...].T
 
     coef = jnp.where(branch == 0, 1.0 - GUIDE, GUIDE).astype(F32)
 
@@ -180,139 +174,155 @@
             for i, dx in enumerate(stat_offsets)
         ]
 
-    def first_pass(turn, _):
-        slot = jnp.where(turn < 2, turn, 5 - turn)
+    def scores(slot, t):
+        q_tile = Q[tile_at(slot, t), :]
+        top = None
+        for i in range(CHUNKS):
+            s = dot(K[chunk(i), :], q_tile, 1, 1)
+            SC[t, chunk(i), :] = s
+            part = jnp.max(eights(s), axis=0)
+            top = part if top is None else jnp.maximum(top, part)
+        return jnp.max(top, axis=0, keepdims=True)
+
+    def sums(slot, t, top):
         chip = lax.rem(x + slot, 4)
-
-        @pl.when(turn == 3)
+        cols = tile_at(slot, t)
+        o_tile = (coef * R[cols, :].astype(F32)).astype(BF)
+        OF[cols, :] = o_tile
+        total, cross = jnp.zeros((8, TILE), F32), jnp.zeros((8, TILE), F32)
+        for i in range(CHUNKS):
+            e = jnp.exp2((SC[t, chunk(i), :] - top) * TO_EXP2)
+            p = dot(V[chunk(i), :], o_tile, 1, 1)
+            E[chunk(i), cols] = e.astype(BF)
+            DP[chunk(i), cols] = p
+            total += jnp.sum(eights(e), axis=0)
+            cross += jnp.sum(eights(e * p), axis=0)
+        ST[chip, 0:1, chunk(t)] = top
+        ST[chip, 1:2, chunk(t)] = jnp.sum(total, axis=0, keepdims=True)
+        ST[chip, 2:3, chunk(t)] = jnp.sum(cross, axis=0, keepdims=True)
+
+    def first_pass(turn, tops):
+        slot = jnp.where(turn == 0, 0, jnp.where(turn == 1, 3, 1))
+        later = jnp.where(turn == 0, 3, jnp.where(turn == 1, 1, 2))
+
+        @pl.when(turn == 1)
+        def _():
+            for half in range(2):
+                wait_r(3, half)
+                wait_q(1, half)
+
+        @pl.when(turn == 2)
         def _():
             for half in range(2):
                 wait_q(2, half)
-                wait_r(2, half)
-
-        def scores(t):
-            q_tile = Q[tile_at(slot, t), :]
-            top = None
-            for i in range(CHUNKS):
-                s = dot(K[chunk(i), :], q_tile, 1, 1)
-                SC[t, chunk(i), :] = s
-                part = jnp.max(eights(s), axis=0)
-                top = part if top is None else jnp.maximum(top, part)
-            return jnp.max(top, axis=0, keepdims=True)
-
-        def sums(t, top):
-            cols = tile_at(slot, t)
-            o_tile = (coef * R[cols, :].astype(F32)).astype(BF)
-            OG[cols, :HEAD_DIM] = o_tile
-            total, cross = jnp.zeros((8, TILE), F32), jnp.zeros((8, TILE), F32)
-            for i in range(CHUNKS):
-                e = jnp.exp2((SC[t, chunk(i), :] - top) * TO_EXP2)
-                p = dot(V[chunk(i), :], o_tile, 1, 1)
-                E[chunk(i), cols] = e.astype(BF)
-                SC[t, chunk(i), :] = e
-                DP[t, chunk(i), :] = p
-                total += jnp.sum(eights(e), axis=0)
-                cross += jnp.sum(eights(e * p), axis=0)
-            total = jnp.sum(total, axis=0, keepdims=True)
-            cross = jnp.sum(cross, axis=0, keepdims=True)
-            ST[chip, 0:1, chunk(t)] = top
-            ST[chip, 1:2, chunk(t)] = total
-            ST[chip, 2:3, chunk(t)] = cross
-            return cross / total
-
-        def grads(t, delta):
-            cols = tile_at(slot, t)
-            for i in range(CHUNKS):
-                ds = SC[t, chunk(i), :] * (DP[t, chunk(i), :] - delta)
-                DS[chunk(i), cols] = ds.astype(BF)
-
-        tops = [scores(0), scores(1)]
-        deltas = [sums(0, tops[0])]
-        tops.append(scores(2))
-        deltas.append(sums(1, tops[1]))
-        grads(0, deltas[0])
-        deltas.append(sums(2, tops[2]))
+
+        new = []
+        for t in range(PER_CHIP):
+            sums(slot, t, tops[t])
+            new.append(scores(later, t))
+        for item in stat_copies(lax.rem(x + slot, 4)):
+            item.start()
+        return tuple(new)
+
+    tops = tuple(scores(0, t) for t in range(PER_CHIP))
+    KT[...] = K[...].T
+    for half in range(2):
+        arrived(V.at[rows_of(1, half)], v_sem.at[1, half])
+    tops = lax.fori_loop(0, 3, first_pass, tops)
+    for half in range(2):
+        wait_r(2, half)
+    for t in range(PER_CHIP):
+        sums(2, t, tops[t])
+    for item in stat_copies(lax.rem(x + 2, 4)):
+        item.start()
+
+    def x_copy(turn, step):
+        slot = jnp.where(turn == 0, 2, jnp.where(turn == 1, 1, 3))
+        half = 1 - branch if step == 0 else branch
+        return copy(
+            PQ.at[rows_of(slot, half)], XB.at[step, turn], x_send.at[step, turn], x_recv.at[step, turn],
+            device(dx=slot),
+        )
+
+    def row_factors(slot):
+        chip = lax.rem(x + slot, 4)
         for item in stat_copies(chip):
-            item.start()
-        grads(1, deltas[1])
-        grads(2, deltas[2])
-        return 0
-
-    lax.fori_loop(0, 4, first_pass, 0)
-
-    def key_products(i, _):
-        cols = pl.ds(pl.multiple_of(i * WIDE, WIDE), WIDE)
-        X[:, cols] = dot(KT[...], DS[:, cols], 1, 0)
-        Y[:, cols] = dot(KT[...], E[:, cols], 1, 0)
-        return 0
-
-    lax.fori_loop(0, NQ // WIDE, key_products, 0)
-
-    for chip in range(4):
-        for item in stat_copies(chip):
-            item.wait()
-        top, total, cross = (ST[chip, k : k + 1, :] for k in range(3))
+            item.wait_recv()
+        top = ST[chip, 0:1, :]
         whole = top
         for i in range(3):
             whole = jnp.maximum(whole, SG[i, chip, 0:1, :])
         here = jnp.exp2((top - whole) * TO_EXP2)
-        total_all, cross_all = here * total, here * cross
+        total_all, cross_all = here * ST[chip, 1:2, :], here * ST[chip, 2:3, :]
         for i in range(3):
             fade = jnp.exp2((SG[i, chip, 0:1, :] - whole) * TO_EXP2)
             total_all += fade * SG[i, chip, 1:2, :]
             cross_all += fade * SG[i, chip, 2:3, :]
-        FD[chip, 0:1, :] = here / total_all
-        FD[chip, 1:2, :] = cross / total - cross_all / total_all
-
-    def second_pass(turn, _):
-        slot = jnp.where(turn == 0, 2, jnp.where(turn == 1, 1, jnp.where(turn == 2, 3, 0)))
-        chip = lax.rem(x + slot, 4)
+        factor = here / total_all
+        FD[slot, 0:1, :] = factor * SCALE
+        FD[slot, 1:2, :] = cross_all / total_all
         for t in range(PER_CHIP):
             cols = tile_at(slot, t)
-            f, shift = FD[chip, 0:1, chunk(t)], FD[chip, 1:2, chunk(t)]
-            part = (X[:, cols] + shift * Y[:, cols]) * (f * SCALE)
-            PQ[cols, :] = part.T.astype(BF)
-            f_col = jnp.broadcast_to(f, (HEAD_DIM, TILE)).T
-            s_col = jnp.broadcast_to(shift, (HEAD_DIM, TILE)).T
-            q_tile = Q[cols, :].astype(F32) * (f_col * SCALE)
-            QF[cols, :] = q_tile.astype(BF)
-            OG[cols, HEAD_DIM:] = (q_tile * s_col).astype(BF)
-            OG[cols, :HEAD_DIM] = (OG[cols, :HEAD_DIM].astype(F32) * f_col).astype(BF)
+            column = jnp.broadcast_to(factor[:, t * TILE : (t + 1) * TILE], (HEAD_DIM, TILE)).T
+            QF[cols, :] = (Q[cols, :].astype(F32) * (column * SCALE)).astype(BF)
+            OF[cols, :] = (OF[cols, :].astype(F32) * column).astype(BF)
+
+    def second_pass(turn):
+        slot = jnp.where(turn == 0, 2, jnp.where(turn == 1, 1, jnp.where(turn == 2, 3, 0)))
+        for t in range(PER_CHIP):
+            cols = tile_at(slot, t)
+            delta = FD[slot, 1:2, chunk(t)]
+            for i in range(CHUNKS):
+                ds = E[chunk(i), cols].astype(F32) * (DP[chunk(i), cols] - delta)
+                DS[chunk(i), cols] = ds.astype(BF)
+        block = pl.ds(pl.multiple_of(slot * CHIP, CHIP), CHIP)
+        part = dot(KT[...], DS[:, block], 1, 0) * FD[slot, 0:1, :]
+        PQ[block, :] = part.T.astype(BF)
+
+    def near_factors(i, _):
+        row_factors(jnp.where(i == 2, 0, 1 + 2 * i))
         return 0
 
-    lax.fori_loop(0, 4, second_pass, 0)
-
-    x_items = []
-    for step, half in enumerate((1 - branch, branch)):
-        for i, dx in enumerate((2, 1, 3)):
-            item = copy(
-                PQ.at[rows_of(dx, half)], XB.at[step, i], x_send.at[step, i], x_recv.at[step, i], device(dx=dx)
+    def near_second(turn, _):
+        second_pass(turn)
+
+        @pl.when(turn < 3)
+        def _():
+            x_copy(turn, 0).start()
+
+        return 0
+
+    def y_copy(i, k):
+        to = device(y_at=lax.rem(y + jnp.where(i == 0, 2, jnp.where(i == 1, 1, 3)), 4))
+        return copy(PKV.at[i, k], YB.at[i, k], y_send.at[i, k], y_recv.at[i, k], to)
+
+    def third_pass(k, scores_ref, factor_ref):
+        def body(i, _):
+            slot = jnp.where((i == 1) | (i == 2), 1, 0)
+            half = jnp.where(
+                i == 0, 1 - branch, jnp.where(i == 1, y_up // 2, jnp.where(i == 2, y_down // 2, branch))
             )
-            item.start()
-            x_items.append(item)
-
-    def y_copy(i):
-        to = device(y_at=lax.rem(y + jnp.where(i == 0, 2, jnp.where(i == 1, 1, 3)), 4))
-        return copy(PKV.at[i], YB.at[i], y_send.at[i], y_recv.at[i], to)
-
-    def third_pass(i, _):
-        slot = jnp.where((i == 1) | (i == 2), 1, 0)
-        half = jnp.where(
-            i == 0, 1 - branch, jnp.where(i == 1, y_up // 2, jnp.where(i == 2, y_down // 2, branch))
-        )
-        rows = rows_of(slot, half)
-        both = dot(E[rows, :], OG[...], 1, 0)
-        grad_k = dot(DS[rows, :], QF[...], 1, 0) + both[:, HEAD_DIM:]
-        PKV[i, 0] = grad_k.astype(BF)
-        PKV[i, 1] = both[:, :HEAD_DIM].astype(BF)
-
-        @pl.when(i < 3)
-        def _():
-            y_copy(i).start()
-
-        return 0
-
-    lax.fori_loop(0, 4, third_pass, 0)
+            grad = dot(scores_ref[rows_of(slot, half), :], factor_ref[...], 1, 0)
+            PKV[i, k] = grad.astype(BF)
+
+            @pl.when(i < 3)
+            def _():
+                y_copy(i, k).start()
+
+            return 0
+
+        lax.fori_loop(0, 4, body, 0)
+
+    row_factors(2)
+    second_pass(0)
+    x_copy(0, 0).start()
+    lax.fori_loop(0, 3, near_factors, 0)
+    third_pass(1, E, OF)
+    lax.fori_loop(1, 4, near_second, 0)
+    for turn in range(3):
+        x_copy(turn, 1).start()
+    third_pass(0, DS, QF)
+    x_items = [x_copy(turn, step) for step in range(2) for turn in range(3)]
 
     def x_sum(step, half):
         total = PQ[rows_of(0, half), :].astype(F32)
@@ -325,9 +335,9 @@
     cross_copy = copy(BX, BR, b_send, b_recv, device(y_at=y_far))
     cross_copy.start()
     total_q = x_sum(1, branch)
-    for i in range(3):
-        arrived(YB.at[i], y_recv.at[i])
-    for k in range(2):
+    for k in (1, 0):
+        for i in range(3):
+            arrived(YB.at[i, k], y_recv.at[i, k])
         total = PKV[3, k].astype(F32)
         for i in range(3):
             total += YB[i, k].astype(F32)
@@ -418,8 +428,12 @@
         item.wait_send()
     for item in x_items:
         item.wait_send()
+    for chip in range(4):
+        for item in stat_copies(chip):
+            item.wait_send()
     for i in range(3):
-        y_copy(i).wait_send()
+        for k in range(2):
+            y_copy(i, k).wait_send()
     cross_copy.wait_send()
     swap.wait_send()
     swap_q.wait_send()
@@ -435,10 +449,9 @@
     sub = FEAT // 2 // SUBS
     scratch = [
         vm(NQ, HEAD_DIM), vm(NQ, HEAD_DIM), vm(NK, HEAD_DIM), vm(NK, HEAD_DIM),
-        vm(HEAD_DIM, NK), vm(NQ, HEAD_DIM), vm(NQ, 2 * HEAD_DIM),
+        vm(HEAD_DIM, NK), vm(NQ, HEAD_DIM), vm(NQ, HEAD_DIM),
         vm(NK, NQ), vm(NK, NQ),
-        vm(PER_CHIP, NK, TILE, dtype=F32), vm(PER_CHIP, NK, TILE, dtype=F32),
-        vm(HEAD_DIM, NQ, dtype=F32), vm(HEAD_DIM, NQ, dtype=F32),
+        vm(PER_CHIP, NK, TILE, dtype=F32), vm(NK, NQ, dtype=F32),
         vm(3, FEAT, 2 * HEAD_DIM),
         vm(4, 8, CHIP, dtype=F32), vm(3, 4, 8, CHIP, dtype=F32), vm(4, 8, CHIP, dtype=F32),
         vm(NQ, HEAD_DIM), vm(4, 2, ROWS, HEAD_DIM),
@@ -448,7 +461,7 @@
         vm(2, 4, 2, SUBS, TOK, sub), vm(2, 3, 2, SUBS, TOK, sub),
         vm(2, 2, SUBS, TOK, sub), vm(TOK, FEAT),
         dma((4, 2)), dma((4, 2)), dma((2, 2)), dma((2, 2)), dma((20,)), dma(()),
-        dma((3, 4)), dma((3, 4)), dma((2, 3)), dma((2, 3)), dma((3,)), dma((3,)),
+        dma((3, 4)), dma((3, 4)), dma((2, 3)), dma((2, 3)), dma((3, 2)), dma((3, 2)),
         dma(()), dma(()), dma((2,)), dma((2,)), dma((2, 4, 2, SUBS)), dma((2, 4, 2, SUBS)), dma(()), dma(()),
     ]
     return pl.pallas_call(

time: 73.8 us -> 69.5 us (0.942)
  Pallas kernels: 72.1 us -> 67.8 us
    pallas_call x1, Pallas kernels: 72.1 us -> 67.8 us  [per_device(): pl.pallas_call(kernel, out_shape=jax.ShapeDtypeStruct((TOK, FEAT), BF), i...]
where the time goes in v3:
time: 69.5 us; the launch traced here: 69.4 us
  Pallas kernels  67.8 us (98%)
  local copies, waits for them, and re-layouts  1.58 us (2%)
    pallas_call x1, Pallas kernels, per_device(): pl.pallas_call(kernel, out_shape=jax.ShapeDtypeStruct((TOK, FEAT), BF), i...  67.8 us
    unnamed x1, local copies, waits for them, and re-layouts  1.58 us

profile of v3, /device:TPU:1, one launch (start us, length us, event | category | flops | bytes accessed | tf_op | source)
XLA Modules:
  0.0 69.4 jit_solution(2526237851442425064)
XLA Ops:
  0.0 67.8 %shard_map.55 = bf16[48,1536]{1,0:T(8,128)(2,1)} custom-call(bf16[1,384,256]{2,1,0:T(8,128)(2,1)} %q_in.1, bf16[1,384,256]{2,1,0:T(8,128)(2,1)} %k_in.1, bf16[1,384,256]{2,1,0:T(8,128)(2,1)} %v_in.1, bf16[384,256]{1,0:T(8,128)(2,1)} %r_in.1, bf16[3,3072,256]{2,1,0:T(8,128)(2,1)} %w_in.1), custom_call_target="tpu_custom_call" | custom-call | tf_op jit(solution)/shard_map/pallas_call | solution.py:467
  67.8 1.6 %copy.7 = bf16[48,1536]{1,0:T(8,128)(2,1)} copy(bf16[48,1536]{1,0:T(8,128)(2,1)} %shard_map.55) | data formatting | bytes 294912

commit v4 on v3

--- a/solution.py
+++ b/solution.py
@@ -283,46 +283,44 @@
         row_factors(jnp.where(i == 2, 0, 1 + 2 * i))
         return 0
 
-    def near_second(turn, _):
-        second_pass(turn)
-
-        @pl.when(turn < 3)
-        def _():
-            x_copy(turn, 0).start()
-
-        return 0
-
     def y_copy(i, k):
         to = device(y_at=lax.rem(y + jnp.where(i == 0, 2, jnp.where(i == 1, 1, 3)), 4))
         return copy(PKV.at[i, k], YB.at[i, k], y_send.at[i, k], y_recv.at[i, k], to)
 
-    def third_pass(k, scores_ref, factor_ref):
-        def body(i, _):
-            slot = jnp.where((i == 1) | (i == 2), 1, 0)
-            half = jnp.where(
-                i == 0, 1 - branch, jnp.where(i == 1, y_up // 2, jnp.where(i == 2, y_down // 2, branch))
-            )
-            grad = dot(scores_ref[rows_of(slot, half), :], factor_ref[...], 1, 0)
-            PKV[i, k] = grad.astype(BF)
-
-            @pl.when(i < 3)
-            def _():
-                y_copy(i, k).start()
-
-            return 0
-
-        lax.fori_loop(0, 4, body, 0)
-
-    row_factors(2)
-    second_pass(0)
-    x_copy(0, 0).start()
-    lax.fori_loop(0, 3, near_factors, 0)
-    third_pass(1, E, OF)
-    lax.fori_loop(1, 4, near_second, 0)
-    for turn in range(3):
-        x_copy(turn, 1).start()
-    third_pass(0, DS, QF)
-    x_items = [x_copy(turn, step) for step in range(2) for turn in range(3)]
+    def third_pass(k, scores_ref, factor_ref, i):
+        slot = jnp.where((i == 1) | (i == 2), 1, 0)
+        half = jnp.where(
+            i == 0, 1 - branch, jnp.where(i == 1, y_up // 2, jnp.where(i == 2, y_down // 2, branch))
+        )
+        grad = dot(scores_ref[rows_of(slot, half), :], factor_ref[...], 1, 0)
+        PKV[i, k] = grad.astype(BF)
+
+        @pl.when(i < 3)
+        def _():
+            y_copy(i, k).start()
+
+    def alternate(i, _):
+        third_pass(1, E, OF, i)
+
+        @pl.when(i < 3)
+        def _():
+            second_pass(i + 1)
+
+        @pl.when(i < 2)
+        def _():
+            x_copy(i + 1, 0).start()
+
+        return 0
+
+    def keys_part(i, _):
+        third_pass(0, DS, QF, i)
+
+        @pl.when(i == 0)
+        def _():
+            BX[...] = x_sum(0, 1 - branch).astype(BF)
+            cross_copy.start()
+
+        return 0
 
     def x_sum(step, half):
         total = PQ[rows_of(0, half), :].astype(F32)
@@ -331,9 +329,16 @@
             total += XB[step, i].astype(F32)
         return total
 
-    BX[...] = x_sum(0, 1 - branch).astype(BF)
     cross_copy = copy(BX, BR, b_send, b_recv, device(y_at=y_far))
-    cross_copy.start()
+    row_factors(2)
+    second_pass(0)
+    x_copy(0, 0).start()
+    lax.fori_loop(0, 3, near_factors, 0)
+    lax.fori_loop(0, 4, alternate, 0)
+    for turn in range(3):
+        x_copy(turn, 1).start()
+    lax.fori_loop(0, 4, keys_part, 0)
+    x_items = [x_copy(turn, step) for step in range(2) for turn in range(3)]
     total_q = x_sum(1, branch)
     for k in (1, 0):
         for i in range(3):

time: 69.5 us -> 68.6 us (0.987)
  Pallas kernels: 67.8 us -> 66.9 us
    pallas_call x1, Pallas kernels: 67.8 us -> 66.9 us  [per_device(): pl.pallas_call(kernel, out_shape=jax.ShapeDtypeStruct((TOK, FEAT), BF), i...]
where the time goes in v4:
time: 68.6 us; the launch traced here: 68.5 us
  Pallas kernels  66.9 us (98%)
  local copies, waits for them, and re-layouts  1.58 us (2%)
    pallas_call x1, Pallas kernels, per_device(): pl.pallas_call(kernel, out_shape=jax.ShapeDtypeStruct((TOK, FEAT), BF), i...  66.9 us
    unnamed x1, local copies, waits for them, and re-layouts  1.58 us

profile of v4, /device:TPU:1, one launch (start us, length us, event | category | flops | bytes accessed | tf_op | source)
XLA Modules:
  0.0 68.5 jit_solution(4530939582558829175)
XLA Ops:
  0.0 66.9 %shard_map.55 = bf16[48,1536]{1,0:T(8,128)(2,1)} custom-call(bf16[1,384,256]{2,1,0:T(8,128)(2,1)} %q_in.1, bf16[1,384,256]{2,1,0:T(8,128)(2,1)} %k_in.1, bf16[1,384,256]{2,1,0:T(8,128)(2,1)} %v_in.1, bf16[384,256]{1,0:T(8,128)(2,1)} %r_in.1, bf16[3,3072,256]{2,1,0:T(8,128)(2,1)} %w_in.1), custom_call_target="tpu_custom_call" | custom-call | tf_op jit(solution)/shard_map/pallas_call | solution.py:472
  66.9 1.6 %copy.7 = bf16[48,1536]{1,0:T(8,128)(2,1)} copy(bf16[48,1536]{1,0:T(8,128)(2,1)} %shard_map.55) | data formatting | bytes 294912

commit v5 on v4

--- a/solution.py
+++ b/solution.py
@@ -43,7 +43,7 @@
     XB, YB, BX, BR, GA, PF, PO, ZB, ZS, ZF, ZO,
     q_sem, r_sem, k_sem, v_sem, g_send, w_sem, st_send, st_recv,
     x_send, x_recv, y_send, y_recv, b_send, b_recv, c_send, c_recv,
-    z_send, z_recv, f_send, f_recv,
+    z_send, z_recv, f_send, f_recv, far_sem,
 ):
     branch = lax.axis_index("branch")
     blk = lax.axis_index("blk")
@@ -79,7 +79,7 @@
     def arrived(dst, recv):
         copy(dst, dst, recv, recv, twin).wait_recv()
 
-    partners = [twin, device(y_at=y_rest), device(y_at=y_far), device(dz=1), device(dz=-1)]
+    partners = [twin, device(y_at=y_rest), device(dz=1), device(dz=-1)]
     for at in (core, other):
         partners += [device(dx=1, core_at=at), device(dx=-1, core_at=at), device(y_at=y_pair, core_at=at)]
     barrier = pltpu.get_barrier_semaphore()
@@ -108,6 +108,7 @@
     ST[...] = jnp.zeros_like(ST)
 
     pl.semaphore_wait(barrier, len(partners))
+    pl.semaphore_signal(far_sem, inc=1, device_id=device(y_at=y_rest), device_id_type=MESH)
 
     sends = []
 
@@ -315,7 +316,7 @@
     def keys_part(i, _):
         third_pass(0, DS, QF, i)
 
-        @pl.when(i == 0)
+        @pl.when(i == 1)
         def _():
             BX[...] = x_sum(0, 1 - branch).astype(BF)
             cross_copy.start()
@@ -334,6 +335,7 @@
     second_pass(0)
     x_copy(0, 0).start()
     lax.fori_loop(0, 3, near_factors, 0)
+    pl.semaphore_wait(far_sem, 1)
     lax.fori_loop(0, 4, alternate, 0)
     for turn in range(3):
         x_copy(turn, 1).start()
@@ -468,6 +470,7 @@
         dma((4, 2)), dma((4, 2)), dma((2, 2)), dma((2, 2)), dma((20,)), dma(()),
         dma((3, 4)), dma((3, 4)), dma((2, 3)), dma((2, 3)), dma((3, 2)), dma((3, 2)),
         dma(()), dma(()), dma((2,)), dma((2,)), dma((2, 4, 2, SUBS)), dma((2, 4, 2, SUBS)), dma(()), dma(()),
+        pltpu.SemaphoreType.REGULAR,
     ]
     return pl.pallas_call(
         kernel,

time: 68.6 us -> 68.6 us (level)
  no operation moved by 1% of the time
where the time goes in v5:
time: 68.6 us; the launch traced here: 68.5 us
  Pallas kernels  66.9 us (98%)
  local copies, waits for them, and re-layouts  1.58 us (2%)
    pallas_call x1, Pallas kernels, per_device(): pl.pallas_call(kernel, out_shape=jax.ShapeDtypeStruct((TOK, FEAT), BF), i...  66.9 us
    unnamed x1, local copies, waits for them, and re-layouts  1.58 us

profile of v5, /device:TPU:1, one launch (start us, length us, event | category | flops | bytes accessed | tf_op | source)
XLA Modules:
  0.0 68.5 jit_solution(18211319888942725407)
XLA Ops:
  0.0 66.9 %shard_map.55 = bf16[48,1536]{1,0:T(8,128)(2,1)} custom-call(bf16[1,384,256]{2,1,0:T(8,128)(2,1)} %q_in.1, bf16[1,384,256]{2,1,0:T(8,128)(2,1)} %k_in.1, bf16[1,384,256]{2,1,0:T(8,128)(2,1)} %v_in.1, bf16[384,256]{1,0:T(8,128)(2,1)} %r_in.1, bf16[3,3072,256]{2,1,0:T(8,128)(2,1)} %w_in.1), custom_call_target="tpu_custom_call" | custom-call | tf_op jit(solution)/shard_map/pallas_call | solution.py:475
  66.9 1.6 %copy.7 = bf16[48,1536]{1,0:T(8,128)(2,1)} copy(bf16[48,1536]{1,0:T(8,128)(2,1)} %shard_map.55) | data formatting | bytes 294912

commit v6 on v5

--- a/solution.py
+++ b/solution.py
@@ -364,8 +364,6 @@
     for i in range(FEAT // TILE):
         PF[:, chunk(i)] = dot(both_heads(1), W[1, chunk(i), :], 1, 1) + dot(both_heads(2), W[2, chunk(i), :], 1, 1)
     arrived(GA.at[other, 0], c_recv.at[1])
-    for i in range(FEAT // TILE):
-        PO[:, chunk(i)] = (PF[:, chunk(i)] + dot(both_heads(0), W[0, chunk(i), :], 1, 1)).astype(BF)
 
     owner_y, owner_core = 2 * core + ylo, branch
     z_to = (device(dz=1), device(dz=-1))
@@ -388,8 +386,10 @@
         item.start()
         z_items.append(item)
 
-    for sub in range(SUBS):
-        for way in range(2):
+    for way in range(2):
+        for i in range(way * FEAT // TILE // 2, (way + 1) * FEAT // TILE // 2):
+            PO[:, chunk(i)] = (PF[:, chunk(i)] + dot(both_heads(0), W[0, chunk(i), :], 1, 1)).astype(BF)
+        for sub in range(SUBS):
             z_start(way, 4, way, sub, z_part(way, 4, way, sub))
     for sub in range(SUBS):
         for way in range(2):

time: 68.6 us -> 68.6 us (level)
  no operation moved by 1% of the time
where the time goes in v6:
time: 68.6 us; the launch traced here: 68.5 us
  Pallas kernels  66.9 us (98%)
  local copies, waits for them, and re-layouts  1.58 us (2%)
    pallas_call x1, Pallas kernels, per_device(): pl.pallas_call(kernel, out_shape=jax.ShapeDtypeStruct((TOK, FEAT), BF), i...  66.9 us
    unnamed x1, local copies, waits for them, and re-layouts  1.58 us

profile of v6, /device:TPU:1, one launch (start us, length us, event | category | flops | bytes accessed | tf_op | source)
XLA Modules:
  0.0 68.5 jit_solution(5189565778395259156)
XLA Ops:
  0.0 66.9 %shard_map.55 = bf16[48,1536]{1,0:T(8,128)(2,1)} custom-call(bf16[1,384,256]{2,1,0:T(8,128)(2,1)} %q_in.1, bf16[1,384,256]{2,1,0:T(8,128)(2,1)} %k_in.1, bf16[1,384,256]{2,1,0:T(8,128)(2,1)} %v_in.1, bf16[384,256]{1,0:T(8,128)(2,1)} %r_in.1, bf16[3,3072,256]{2,1,0:T(8,128)(2,1)} %w_in.1), custom_call_target="tpu_custom_call" | custom-call | tf_op jit(solution)/shard_map/pallas_call | solution.py:475
  66.9 1.6 %copy.7 = bf16[48,1536]{1,0:T(8,128)(2,1)} copy(bf16[48,1536]{1,0:T(8,128)(2,1)} %shard_map.55) | data formatting | bytes 294912
